TPU v7x, 256 devices: a whole 4x4x8 slice. The times are simulated.
256 devices in a mesh: gx: 32 (over y, x, core), gy: 8 (over z).
Axes of the slice: x: 4, y: 4, z: 8, core: 2. Of those that a mesh axis runs over, the one named last changes fastest.
Arguments:
- embeddings: bfloat16 [262144, 1024], P(('gx', 'gy')), may hold values from -60 to 60
- cluster: int32 [262144], replicated, may hold values from 0 to 511, never falling along the last dimension, each value on 1 to 4096 neighbouring positions
Outputs:
- log_cover: float32 [262144], P(('gx', 'gy'))
- relative_cover: float32 [262144], P(('gx', 'gy'))
Inputs may be any that keep to these rules, and one draw needn't show every extreme that they name: cluster numbers never fall along the rows; each cluster holds 1 to 4096 rows and one holds exactly that many.
All inputs are finite; a program needn't handle non-finite values.
Results may differ from a plain program's by a relative error of at most 0.002.
Values may be sent and summed in bfloat16 or wider, within the bound.
A program may use at most 64 MiB of HBM per device.

v0:
```python
import jax
import jax.numpy as jnp
from jax import lax
from jax.sharding import PartitionSpec as P

REACH = 4


INVERSE_TEMP = 100.0
FLOOR_SCORE = -1e30
EPSILON = 1e-06


def passed_along(shard, axis, by):
    peers = lax.axis_size(axis)
    pairs = [(i, i + by) for i in range(peers) if 0 <= i + by < peers]
    return lax.ppermute(shard, axis, pairs)


def unit_rows(embeddings):
    values = embeddings.astype(jnp.float32)
    scale = lax.rsqrt(jnp.sum(values * values, axis=1, keepdims=True) + EPSILON)
    return (values * scale).astype(jnp.bfloat16)


def combine(first, second):
    top = jnp.maximum(first[0], second[0])
    total = first[1] * jnp.exp(first[0] - top) + second[1] * jnp.exp(second[0] - top)
    return (top, total)


def tile_parts(left_block, right_block, left_tags, right_tags, diagonal):
    scores = (
        lax.dot_general(
            left_block, right_block, (((1,), (1,)), ((), ())), preferred_element_type=jnp.float32
        )
        * INVERSE_TEMP
    )
    is_live = left_tags[:, None] == right_tags[None, :]
    if diagonal:
        size_rows = left_block.shape[0]
        is_live = is_live & (jnp.arange(size_rows)[:, None] != jnp.arange(size_rows)[None, :])
    masked = jnp.where(is_live, scores, FLOOR_SCORE)
    row_max = jnp.max(masked, axis=1)
    col_max = jnp.max(masked, axis=0)
    row_sum = jnp.sum(jnp.where(is_live, jnp.exp(masked - row_max[:, None]), 0.0), axis=1)
    col_sum = jnp.sum(jnp.where(is_live, jnp.exp(masked - col_max[None, :]), 0.0), axis=0)
    return ((row_max, row_sum), (col_max, col_sum))


def finish(part):
    top = jnp.maximum(part[0], 0.0)
    return top + jnp.log(jnp.exp(-top) + part[1] * jnp.exp(part[0] - top))


def per_device(embeddings, cluster):
    block_rows = embeddings.shape[0]
    cluster_count = 2 * lax.axis_size("gx") * lax.axis_size("gy")
    unit_block = unit_rows(embeddings)
    device_place = lax.axis_index(("gx", "gy"))
    pad_tags = jnp.concatenate([cluster + 1, jnp.zeros((REACH * block_rows,), jnp.int32)], axis=0)

    def tags_at(offset):
        first_row = (device_place + offset) * block_rows
        return lax.dynamic_slice_in_dim(pad_tags, first_row, block_rows, 0)

    own_tags = tags_at(0)
    far_blocks = [passed_along(unit_block, ("gx", "gy"), -offset) for offset in range(1, REACH + 1)]
    row_part, unused = tile_parts(unit_block, unit_block, own_tags, own_tags, True)
    for offset in range(1, REACH + 1):
        far_tags = tags_at(offset)
        right_block = far_blocks[offset - 1]
        side_row, side_col = tile_parts(unit_block, right_block, own_tags, far_tags, False)
        row_part = combine(row_part, side_row)
        arrived = passed_along((side_col[0], side_col[1]), ("gx", "gy"), offset)
        row_part = combine(row_part, arrived)
    log_cover = finish(row_part)
    onehot = (
        cluster_slice(cluster, device_place, block_rows)[:, None]
        == jnp.arange(cluster_count, dtype=jnp.int32)[None, :]
    ).astype(jnp.float32)
    local_sums = jnp.dot(log_cover, onehot, precision=lax.Precision.HIGHEST)
    local_counts = jnp.sum(onehot, axis=0)
    cluster_sums, cluster_counts = lax.psum((local_sums, local_counts), ("gx", "gy"))
    cluster_mean = cluster_sums / jnp.maximum(cluster_counts, 1.0)
    row_mean = jnp.dot(onehot, cluster_mean, precision=lax.Precision.HIGHEST)
    return (log_cover, log_cover - row_mean)


def cluster_slice(cluster, device_place, block_rows):
    first_row = device_place * block_rows
    return lax.dynamic_slice_in_dim(cluster, first_row, block_rows, 0)


def solution(mesh):
    placed = (P(("gx", "gy"), None), P())
    return jax.shard_map(
        per_device,
        mesh=mesh,
        in_specs=placed,
        out_specs=(P(("gx", "gy")), P(("gx", "gy"))),
        check_vma=False,
    )
```

profile of v0, /device:TPU:32, one launch (start us, length us, event | category | flops | bytes accessed | tf_op | source)
XLA Modules:
  0.0 501.9 jit_solution(4164465637568675322)
XLA Ops:
  0.6 2.2 fusion
  2.8 2.0 fusion.1
  4.8 1.3 collective-permute-start.4
  6.1 1.3 collective-permute-start.2
  7.4 1.3 collective-permute-start.6
  8.7 3.8 collective-permute-start
  12.5 0.1 broadcast_add_fusion
  12.6 114.8 %collective-permute-done.4 = bf16[1024,1024]{1,0:T(8,128)(2,1)} collective-permute-done((bf16[1024,1024]{1,0:T(8,128)(2,1)S(1)}, bf16[1024,1024]{1,0:T(8,128)(2,1)}, u32[]{:S(2)}, u32[]{:S(2)}) %collective-permute-start.4) | collective-permute-done | bytes 2097184 | tf_op jit(solution)/shard_map/ppermute | solution.py:17
  127.4 4.3 fusion.39
  131.7 62.8 %collective-permute-done.2 = bf16[1024,1024]{1,0:T(8,128)(2,1)} collective-permute-done((bf16[1024,1024]{1,0:T(8,128)(2,1)S(1)}, bf16[1024,1024]{1,0:T(8,128)(2,1)}, u32[]{:S(2)}, u32[]{:S(2)}) %collective-permute-start.2) | collective-permute-done | bytes 2097184 | tf_op jit(solution)/shard_map/ppermute | solution.py:17
  194.5 4.3 fusion.38
  198.7 130.7 %collective-permute-done.6 = bf16[1024,1024]{1,0:T(8,128)(2,1)} collective-permute-done((bf16[1024,1024]{1,0:T(8,128)(2,1)S(1)}, bf16[1024,1024]{1,0:T(8,128)(2,1)}, u32[]{:S(2)}, u32[]{:S(2)}) %collective-permute-start.6) | collective-permute-done | bytes 2097184 | tf_op jit(solution)/shard_map/ppermute | solution.py:17
  329.5 4.3 fusion.40
  333.7 3.9 fusion.6
  337.6 4.3 fusion.37
  341.9 8.0 %fusion.2 = (f32[1024]{0:T(1024)S(1)}, f32[1024]{0:T(1024)S(1)}, f32[1024]{0:T(1024)S(1)}, f32[1024]{0:T(1024)S(1)}, f32[1024]{0:T(1024)S(1)}, /*index=5*/f32[1024]{0:T(1024)S(1)}, f32[1024]{0:T(1024)S(1)}) fusion(f32[1024,1024]{0,1:T(8,128)S(1)} %get-tuple-element.32, f32[1024]{0:T(1024)S(1)} %get-tuple-element.10, s32[1024]{0:T(1024)S(1)} %get-tuple-element.31, ...), kind=kLoop, calls=%fused_computation.16 | loop fusion | flops 30401536 | bytes 16850944 | tf_op jit(solution)/shard_map/reduce_sum | solution.py:46
  349.9 37.2 %collective-permute-start.11 = (f32[1024]{0:T(1024)S(1)}, f32[1024]{0:T(1024)S(1)}, u32[]{:S(2)}, u32[]{:S(2)}) collective-permute-start(f32[1024]{0:T(1024)S(1)} %get-tuple-element.21), channel_id=1, source_target_pairs={{0,4},{1,5},{2,6},{3,7},{4,8},{5,9},{6,10},{7,11},{8,12},{9,13},{1... | collective-permute-start | bytes 12296 | tf_op jit(solution)/shard_map/ppermute | solution.py:17
  387.1 1.9 collective-permute-start.8
  389.0 3.6 collective-permute-start.9
  392.6 0.7 dynamic_slice.23
  393.3 1.9 collective-permute-start.3
  395.2 6.5 %collective-permute-start.5 = (f32[1024]{0:T(1024)S(1)}, f32[1024]{0:T(1024)S(1)}, u32[]{:S(2)}, u32[]{:S(2)}) collective-permute-start(f32[1024]{0:T(1024)S(1)} %get-tuple-element.15), channel_id=1, source_target_pairs={{0,3},{1,4},{2,5},{3,6},{4,7},{5,8},{6,9},{7,10},{8,11},{9,12},{10... | collective-permute-start | bytes 12296 | tf_op jit(solution)/shard_map/ppermute | solution.py:17
  401.8 8.7 %collective-permute-start.7 = (f32[1024]{0:T(1024)S(1)}, f32[1024]{0:T(1024)S(1)}, u32[]{:S(2)}, u32[]{:S(2)}) collective-permute-start(f32[1024]{0:T(1024)S(1)} %get-tuple-element.17), channel_id=1, source_target_pairs={{0,4},{1,5},{2,6},{3,7},{4,8},{5,9},{6,10},{7,11},{8,12},{9,13},{1... | collective-permute-start | bytes 12296 | tf_op jit(solution)/shard_map/ppermute | solution.py:17
  410.5 2.5 collective-permute-start.1
  413.0 5.8 %collective-permute-start.10 = (f32[1024]{0:T(1024)S(1)}, f32[1024]{0:T(1024)S(1)}, u32[]{:S(2)}, u32[]{:S(2)}) collective-permute-start(f32[1024]{0:T(1024)S(1)} %get-tuple-element.7), channel_id=1, source_target_pairs={{0,3},{1,4},{2,5},{3,6},{4,7},{5,8},{6,9},{7,10},{8,11},{9,12},{10... | collective-permute-start | bytes 12296 | tf_op jit(solution)/shard_map/ppermute | solution.py:17
  418.8 0.3 convert_reduce_fusion
  419.1 1.0 collective-permute-done.10
  420.1 0.0 copy-start.1
  420.2 0.8 fusion.13
  421.0 79.3 %all-reduce.1 = (f32[512]{0:T(512)S(1)}, f32[512]{0:T(512)S(1)}) all-reduce(f32[512]{0:T(512)S(1)} %bitcast.19, f32[512]{0:T(512)S(1)} %convert_reduce_fusion), channel_id=1, replica_groups=mesh['gx'=32,'gy'=8] {'gx','gy'}, use_global_device_ids=true, to_apply=%region_19.20 | all-reduce | flops 1024 | bytes 8192 | tf_op jit(solution)/shard_map/psum | solution.py:84
  500.3 1.1 fusion.12
  501.3 0.6 sub.161
  (15 shorter events, 0.1 us)
Async XLA Ops:
  0.6 11.9 %copy-start = (s32[262144]{0:T(1024)S(1)}, s32[262144]{0:T(1024)}, u32[]{:S(2)}) copy-start(s32[262144]{0:T(1024)} %param.3) | copy-start | bytes 3145732
  4.8 122.6 %collective-permute-start.4 = (bf16[1024,1024]{1,0:T(8,128)(2,1)S(1)}, bf16[1024,1024]{1,0:T(8,128)(2,1)}, u32[]{:S(2)}, u32[]{:S(2)}) collective-permute-start(bf16[1024,1024]{1,0:T(8,128)(2,1)S(1)} %fusion.1), channel_id=1, source_target_pairs={{3,0},{4,1},{5,2},{6,3},{7,4},{8,5},{9,6},{10,7},{11,8},{12,9},{13... | collective-permute-start | bytes 6291464 | tf_op jit(solution)/shard_map/ppermute | solution.py:17
  6.1 188.4 %collective-permute-start.2 = (bf16[1024,1024]{1,0:T(8,128)(2,1)S(1)}, bf16[1024,1024]{1,0:T(8,128)(2,1)}, u32[]{:S(2)}, u32[]{:S(2)}) collective-permute-start(bf16[1024,1024]{1,0:T(8,128)(2,1)S(1)} %fusion.1), channel_id=1, source_target_pairs={{2,0},{3,1},{4,2},{5,3},{6,4},{7,5},{8,6},{9,7},{10,8},{11,9},{12,... | collective-permute-start | bytes 6291464 | tf_op jit(solution)/shard_map/ppermute | solution.py:17
  7.4 322.0 %collective-permute-start.6 = (bf16[1024,1024]{1,0:T(8,128)(2,1)S(1)}, bf16[1024,1024]{1,0:T(8,128)(2,1)}, u32[]{:S(2)}, u32[]{:S(2)}) collective-permute-start(bf16[1024,1024]{1,0:T(8,128)(2,1)S(1)} %fusion.1), channel_id=1, source_target_pairs={{4,0},{5,1},{6,2},{7,3},{8,4},{9,5},{10,6},{11,7},{12,8},{13,9},{1... | collective-permute-start | bytes 6291464 | tf_op jit(solution)/shard_map/ppermute | solution.py:17
  8.7 328.9 %collective-permute-start = (bf16[1024,1024]{1,0:T(8,128)(2,1)S(1)}, bf16[1024,1024]{1,0:T(8,128)(2,1)}, u32[]{:S(2)}, u32[]{:S(2)}) collective-permute-start(bf16[1024,1024]{1,0:T(8,128)(2,1)S(1)} %fusion.1), channel_id=1, source_target_pairs={{1,0},{2,1},{3,2},{4,3},{5,4},{6,5},{7,6},{8,7},{9,8},{10,9},{11,1... | collective-permute-start | bytes 6291464 | tf_op jit(solution)/shard_map/ppermute | solution.py:17
  349.9 51.9 %collective-permute-start.11 = (f32[1024]{0:T(1024)S(1)}, f32[1024]{0:T(1024)S(1)}, u32[]{:S(2)}, u32[]{:S(2)}) collective-permute-start(f32[1024]{0:T(1024)S(1)} %get-tuple-element.21), channel_id=1, source_target_pairs={{0,4},{1,5},{2,6},{3,7},{4,8},{5,9},{6,10},{7,11},{8,12},{9,13},{1... | collective-permute-start | bytes 12296 | tf_op jit(solution)/shard_map/ppermute | solution.py:17
  387.1 23.4 %collective-permute-start.8 = (f32[1024]{0:T(1024)S(1)}, f32[1024]{0:T(1024)S(1)}, u32[]{:S(2)}, u32[]{:S(2)}) collective-permute-start(f32[1024]{0:T(1024)S(1)} %get-tuple-element.3), channel_id=1, source_target_pairs={{0,1},{1,2},{2,3},{3,4},{4,5},{5,6},{6,7},{7,8},{8,9},{9,10},{10,1... | collective-permute-start | bytes 12296 | tf_op jit(solution)/shard_map/ppermute | solution.py:17
  389.0 23.9 %collective-permute-start.9 = (f32[1024]{0:T(1024)S(1)}, f32[1024]{0:T(1024)S(1)}, u32[]{:S(2)}, u32[]{:S(2)}) collective-permute-start(f32[1024]{0:T(1024)S(1)} %get-tuple-element.23), channel_id=1, source_target_pairs={{0,2},{1,3},{2,4},{3,5},{4,6},{5,7},{6,8},{7,9},{8,10},{9,11},{10,... | collective-permute-start | bytes 12296 | tf_op jit(solution)/shard_map/ppermute | solution.py:17
  393.3 26.8 %collective-permute-start.3 = (f32[1024]{0:T(1024)S(1)}, f32[1024]{0:T(1024)S(1)}, u32[]{:S(2)}, u32[]{:S(2)}) collective-permute-start(f32[1024]{0:T(1024)S(1)} %get-tuple-element.13), channel_id=1, source_target_pairs={{0,2},{1,3},{2,4},{3,5},{4,6},{5,7},{6,8},{7,9},{8,10},{9,11},{10,... | collective-permute-start | bytes 12296 | tf_op jit(solution)/shard_map/ppermute | solution.py:17
  395.2 24.8 %collective-permute-start.5 = (f32[1024]{0:T(1024)S(1)}, f32[1024]{0:T(1024)S(1)}, u32[]{:S(2)}, u32[]{:S(2)}) collective-permute-start(f32[1024]{0:T(1024)S(1)} %get-tuple-element.15), channel_id=1, source_target_pairs={{0,3},{1,4},{2,5},{3,6},{4,7},{5,8},{6,9},{7,10},{8,11},{9,12},{10... | collective-permute-start | bytes 12296 | tf_op jit(solution)/shard_map/ppermute | solution.py:17
  401.8 18.3 %collective-permute-start.7 = (f32[1024]{0:T(1024)S(1)}, f32[1024]{0:T(1024)S(1)}, u32[]{:S(2)}, u32[]{:S(2)}) collective-permute-start(f32[1024]{0:T(1024)S(1)} %get-tuple-element.17), channel_id=1, source_target_pairs={{0,4},{1,5},{2,6},{3,7},{4,8},{5,9},{6,10},{7,11},{8,12},{9,13},{1... | collective-permute-start | bytes 12296 | tf_op jit(solution)/shard_map/ppermute | solution.py:17
  410.5 9.6 %collective-permute-start.1 = (f32[1024]{0:T(1024)S(1)}, f32[1024]{0:T(1024)S(1)}, u32[]{:S(2)}, u32[]{:S(2)}) collective-permute-start(f32[1024]{0:T(1024)S(1)} %get-tuple-element.11), channel_id=1, source_target_pairs={{0,1},{1,2},{2,3},{3,4},{4,5},{5,6},{6,7},{7,8},{8,9},{9,10},{10,1... | collective-permute-start | bytes 12296 | tf_op jit(solution)/shard_map/ppermute | solution.py:17
  413.0 7.1 %collective-permute-start.10 = (f32[1024]{0:T(1024)S(1)}, f32[1024]{0:T(1024)S(1)}, u32[]{:S(2)}, u32[]{:S(2)}) collective-permute-start(f32[1024]{0:T(1024)S(1)} %get-tuple-element.7), channel_id=1, source_target_pairs={{0,3},{1,4},{2,5},{3,6},{4,7},{5,8},{6,9},{7,10},{8,11},{9,12},{10... | collective-permute-start | bytes 12296 | tf_op jit(solution)/shard_map/ppermute | solution.py:17
  420.1 81.8 %copy-start.1 = (f32[1024]{0:T(1024)}, f32[1024]{0:T(1024)S(1)}, u32[]{:S(2)}) copy-start(f32[1024]{0:T(1024)S(1)} %maximum_add_fusion) | copy-start | bytes 12292
where the time goes:
time: 503 us; the launch traced here: 502 us
  waiting for transfers between devices  309 us (61%)
  blocking collectives  79.3 us (16%)
  starting transfers between devices  75.7 us (15%)
  matrix products  22.8 us (5%)
  other arithmetic  13.2 us (3%)
    ppermute x12, waiting for transfers between devices, passed_along(): return lax.ppermute(shard, axis, pairs)  309 us
    psum x1, blocking collectives, per_device(): lax.psum((local_sums, local_counts), ('gx', 'gy'))  79.3 us
    ppermute x12, starting transfers between devices, passed_along(): return lax.ppermute(shard, axis, pairs)  75.7 us
    dot_general x5, matrix products, tile_parts(): lax.dot_general(left_block, right_block, (((1,), (1,)), ((), ())), prefer...  20.9 us
  transfers between devices with their start and end apart: 12, of which 4 were waited for; matrix products, arithmetic and copies ran while one was open for 4% of the time, Pallas kernels for 0%

commit v1 on v0

v1 whole, which is shorter than its diff:
```python
import math

import jax
import jax.numpy as jnp
from jax import lax
from jax.experimental import pallas as pl
from jax.experimental.pallas import tpu as pltpu
from jax.sharding import PartitionSpec as P

MESH = pl.DeviceIdType.MESH
INVERSE_TEMP = 100.0
EPSILON = 1e-06
SHIFT = 32.0
GAIN = INVERSE_TEMP * math.log2(math.e)
DROP = SHIFT * math.log2(math.e)

ROWS = 1024
CHUNK = 128
CHUNKS = ROWS // CHUNK
LEFT, RIGHT = 0, 1
REACH = 4


def chunk_rows(c):
    return pl.ds(pl.multiple_of(c * CHUNK, CHUNK), CHUNK)


def across(row):
    return jnp.transpose(jnp.broadcast_to(row, (CHUNK, CHUNK)))


def scores_of(left, right):
    return lax.dot_general(left, right, (((1,), (1,)), ((), ())), preferred_element_type=jnp.float32)


def kernel(
    x_ref, cluster_ref, cover_ref, relative_ref,
    raw, own, near, far, tags, columns, row_sums, col_sums, parts, parts_in, sums, sums_in,
    raw_sem, tags_sem, own_send, relay_send, near_recv, far_recv, parts_send, parts_recv, sums_send, sums_recv,
):
    sizes = (lax.axis_size("gx"), lax.axis_size("gy"))
    devices = sizes[0] * sizes[1]
    me = lax.axis_index("gx") * sizes[1] + lax.axis_index("gy")

    def block(offset):
        return lax.rem(me + (offset + devices), devices)

    def device(offset):
        place = block(offset)
        return (place // sizes[1], lax.rem(place, sizes[1]))

    def raw_copy(c):
        return pltpu.make_async_copy(x_ref.at[chunk_rows(c)], raw.at[chunk_rows(c)], raw_sem.at[c])

    def tags_copy(k):
        return pltpu.make_async_copy(cluster_ref.at[block(k - REACH)], tags.at[k], tags_sem.at[k])

    def own_copy(side, c):
        return pltpu.make_async_remote_copy(
            src_ref=own.at[chunk_rows(c)], dst_ref=near.at[side, chunk_rows(c)],
            send_sem=own_send.at[side, c], recv_sem=near_recv.at[side, c],
            device_id=device(1 if side == LEFT else -1), device_id_type=MESH,
        )

    def relay_copy(side, c):
        return pltpu.make_async_remote_copy(
            src_ref=near.at[side, chunk_rows(c)], dst_ref=far.at[side, chunk_rows(c)],
            send_sem=relay_send.at[side, c], recv_sem=far_recv.at[side, c],
            device_id=device(1 if side == LEFT else -1), device_id_type=MESH,
        )

    steps = [7, 0, 6, 1, 5, 2, 4, 3]
    for c in steps:
        raw_copy(c).start()
    for k in range(2 * REACH + 1):
        tags_copy(k).start()

    barrier = pltpu.get_barrier_semaphore()
    others = [k for k in range(-REACH, REACH + 1) if k != 0]
    for k in others:
        pl.semaphore_signal(barrier, inc=1, device_id=device(k), device_id_type=MESH)
    row_sums[...] = jnp.zeros_like(row_sums)
    col_sums[...] = jnp.zeros_like(col_sums)

    def normalise(c):
        raw_copy(c).wait()

        def some(g, carry):
            rows = pl.ds(pl.multiple_of(c * CHUNK + g * 16, 16), 16)
            values = raw[rows].astype(jnp.float32)
            scale = lax.rsqrt(jnp.sum(values * values, axis=1, keepdims=True) + EPSILON)
            own[rows] = (values * scale).astype(jnp.bfloat16)
            return carry

        lax.fori_loop(0, CHUNK // 16, some, 0, unroll=2)

    normalise(7)
    normalise(0)
    pl.semaphore_wait(barrier, len(others))
    own_copy(LEFT, 7).start()
    own_copy(RIGHT, 0).start()
    for n in range(1, 4):
        normalise(7 - n)
        normalise(n)
        own_copy(LEFT, 7 - n).start()
        own_copy(RIGHT, n).start()
    for n in range(4, CHUNKS):
        own_copy(LEFT, 7 - n).start()
        own_copy(RIGHT, n).start()

    for k in range(2 * REACH + 1):
        tags_copy(k).wait()

    def columns_of(c, carry):
        for k in range(5):
            columns[k, chunk_rows(c)] = across(tags[k + 2, pl.ds(c, 1), :])
        return carry

    lax.fori_loop(0, CHUNKS, columns_of, 0)

    def piece(down, down_tags, right_ref, tag_row, first, width, row_at, col_at, same=None):
        right = right_ref[pl.ds(pl.multiple_of(first * CHUNK, CHUNK), width * CHUNK)]
        scores = scores_of(down, right)
        total = None
        for w in range(width):
            live = down_tags == tags[tag_row, pl.ds(first + w, 1), :]
            if same is not None:
                distinct = lax.broadcasted_iota(jnp.int32, (CHUNK, CHUNK), 0) + (same - (first + w)) * CHUNK
                live = live & (distinct != lax.broadcasted_iota(jnp.int32, (CHUNK, CHUNK), 1))
            cover = jnp.where(live, jnp.exp2(scores[:, w * CHUNK : (w + 1) * CHUNK] * GAIN - DROP), 0.0)
            if row_at is not None:
                total = cover if total is None else total + cover
            col_sums[col_at, first + w] += jnp.sum(cover.reshape(CHUNK // 8, 8, CHUNK), axis=0)
        if row_at is not None:
            which, c = row_at
            row_sums[which, chunk_rows(c)] += total

    def strip(down_ref, down_at, c, right_ref, right_at, row_which, col_at, diagonal=False):
        down = down_ref[chunk_rows(c)]
        down_tags = columns[down_at + 2, chunk_rows(c)]
        for first in range(0, CHUNKS, 2):
            piece(
                down, down_tags, right_ref, right_at + REACH, first, 2,
                None if row_which is None else (row_which, c), col_at, c if diagonal else None,
            )

    left1, left2, right1, right2 = near.at[LEFT], far.at[LEFT], near.at[RIGHT], far.at[RIGHT]
    ROW_L1, ROW_R1, ROW_R2 = 0, 1, 2
    COL_S, COL_L1, COL_L2 = 0, 1, 2

    def diagonal_step(c, carry):
        strip(own, 0, c, own, 0, None, COL_S, diagonal=True)
        return carry

    lax.fori_loop(0, CHUNKS, diagonal_step, 0)

    def near_step(n, carry):
        own_copy(LEFT, 7 - n).wait_recv()
        relay_copy(LEFT, 7 - n).start()
        own_copy(RIGHT, n).wait_recv()
        relay_copy(RIGHT, n).start()
        strip(left1, -1, 7 - n, own, 0, ROW_L1, COL_S)
        return carry

    lax.fori_loop(0, CHUNKS, near_step, 0)

    def middle_step(c, carry):
        strip(right1, 1, c, left1, -1, ROW_R1, COL_L1)
        return carry

    lax.fori_loop(0, CHUNKS, middle_step, 0)

    def corner(c, d):
        piece(right2[chunk_rows(c)], columns[4, chunk_rows(c)], left2, REACH - 2, d, 1, (ROW_R2, c), COL_L2)

    def far_step(n, carry):
        relay_copy(RIGHT, n).wait_recv()
        strip(right2, 2, n, left1, -1, ROW_R2, COL_L1)
        relay_copy(LEFT, 7 - n).wait_recv()

        def new_right(d, inner):
            corner(n, d)
            return inner

        def new_left(c, inner):
            corner(c, 7 - n)
            return inner

        lax.fori_loop(jnp.maximum(n, 7 - n), CHUNKS, new_right, 0)
        lax.fori_loop(0, jnp.minimum(n, 8 - n), new_left, 0)
        return carry

    lax.fori_loop(0, CHUNKS, far_step, 0)

    for c in range(CHUNKS):
        rows = slice(c * CHUNK, (c + 1) * CHUNK)
        lane = slice(c, c + 1)
        down = [jnp.sum(jnp.transpose(row_sums[k, rows]), axis=0, keepdims=True) for k in range(3)]
        side = [jnp.sum(col_sums[k, c], axis=0, keepdims=True) for k in range(3)]
        parts[0, lane] = side[COL_L2]
        parts[1, lane] = down[ROW_L1] + side[COL_L1]
        parts[2, lane] = down[ROW_R1]
        parts[3, lane] = down[ROW_R2]
        parts[4, lane] = side[COL_S]

    part_offsets = [-2, -1, 1, 2]

    def parts_copy(k):
        return pltpu.make_async_remote_copy(
            src_ref=parts.at[k], dst_ref=parts_in.at[k], send_sem=parts_send.at[k], recv_sem=parts_recv.at[k],
            device_id=device(part_offsets[k]), device_id_type=MESH,
        )

    for k in range(4):
        parts_copy(k).start()

    mine = tags[REACH]
    zero = jnp.zeros((CHUNKS, CHUNK), jnp.float32)

    def edge_tag(k):
        at = tags[k + REACH, CHUNKS - 1 : CHUNKS, CHUNK - 1 : CHUNK] if k < 0 else tags[k + REACH, 0:1, 0:1]
        return jnp.broadcast_to(at, (CHUNKS, CHUNK))

    def total_of(values):
        return jnp.broadcast_to(jnp.sum(values, keepdims=True), (CHUNKS, CHUNK))

    def own_totals(column_values):
        totals = []
        for j in range(CHUNKS):

            def add(c, acc):
                same = columns[2, chunk_rows(c)] == tags[REACH, j : j + 1, :]
                picked = jnp.where(same, column_values(c), 0.0)
                return acc + jnp.sum(picked.reshape(CHUNK // 8, 8, CHUNK), axis=0)

            acc = lax.fori_loop(0, CHUNKS, add, jnp.zeros((8, CHUNK), jnp.float32), unroll=True)
            totals.append(jnp.sum(acc, axis=0, keepdims=True))
        return jnp.concatenate(totals, axis=0)

    counts = own_totals(lambda c: 1.0)
    for k in others:
        edge = edge_tag(k)
        many = total_of(jnp.where(tags[k + REACH] == edge, 1.0, 0.0))
        counts = counts + jnp.where(mine == edge, many, 0.0)

    total = parts[4]
    for k in range(4):
        parts_copy(k).wait_recv()
        total = total + parts_in[k]
    cover = jnp.where(
        total < math.exp(-SHIFT),
        jnp.log1p(jnp.minimum(total, math.exp(-SHIFT)) * math.exp(SHIFT)),
        SHIFT + jnp.log(total + math.exp(-SHIFT)),
    )
    cover_ref[...] = cover

    first_tag = jnp.broadcast_to(mine[0:1, 0:1], (CHUNKS, CHUNK))
    last_tag = jnp.broadcast_to(mine[CHUNKS - 1 : CHUNKS, CHUNK - 1 : CHUNK], (CHUNKS, CHUNK))
    sums[0] = total_of(jnp.where(mine == first_tag, cover, zero))
    sums[1] = total_of(jnp.where(mine == last_tag, cover, zero))

    def sums_copy(k):
        at = others.index(k)
        return pltpu.make_async_remote_copy(
            src_ref=sums.at[0 if k < 0 else 1], dst_ref=sums_in.at[at], send_sem=sums_send.at[at], recv_sem=sums_recv.at[at],
            device_id=device(k), device_id_type=MESH,
        )

    for k in others:
        sums_copy(k).start()
    for c in range(CHUNKS):
        row_sums[0, c * CHUNK : (c + 1) * CHUNK] = across(cover[c : c + 1])
    cluster_sums = own_totals(lambda c: row_sums[0, chunk_rows(c)])
    for k in others:
        sums_copy(k).wait_recv()
        cluster_sums = cluster_sums + jnp.where(mine == edge_tag(-k), sums_in[others.index(k)], zero)
    relative_ref[...] = cover - cluster_sums / counts

    for side in (LEFT, RIGHT):
        for c in range(CHUNKS):
            own_copy(side, c).wait_send()
            relay_copy(side, c).wait_send()
    for k in range(4):
        parts_copy(k).wait_send()
    for k in others:
        sums_copy(k).wait_send()


def per_device(embeddings, cluster):
    rows, width = embeddings.shape
    vmem = pl.BlockSpec(memory_space=pltpu.VMEM)
    anywhere = pl.BlockSpec(memory_space=pltpu.HBM)
    dma = pltpu.SemaphoreType.DMA
    cover, relative = pl.pallas_call(
        kernel,
        out_shape=[jax.ShapeDtypeStruct((CHUNKS, CHUNK), jnp.float32)] * 2,
        in_specs=[anywhere, anywhere],
        out_specs=[vmem, vmem],
        scratch_shapes=[
            pltpu.VMEM((rows, width), jnp.bfloat16),
            pltpu.VMEM((rows, width), jnp.bfloat16),
            pltpu.VMEM((2, rows, width), jnp.bfloat16),
            pltpu.VMEM((2, rows, width), jnp.bfloat16),
            pltpu.VMEM((2 * REACH + 1, CHUNKS, CHUNK), jnp.int32),
            pltpu.VMEM((5, rows, CHUNK), jnp.int32),
            pltpu.VMEM((3, rows, CHUNK), jnp.float32),
            pltpu.VMEM((3, CHUNKS, 8, CHUNK), jnp.float32),
            pltpu.VMEM((5, CHUNKS, CHUNK), jnp.float32),
            pltpu.VMEM((4, CHUNKS, CHUNK), jnp.float32),
            pltpu.VMEM((2, CHUNKS, CHUNK), jnp.float32),
            pltpu.VMEM((2 * REACH, CHUNKS, CHUNK), jnp.float32),
            dma((CHUNKS,)),
            dma((2 * REACH + 1,)),
            dma((2, CHUNKS)),
            dma((2, CHUNKS)),
            dma((2, CHUNKS)),
            dma((2, CHUNKS)),
            dma((4,)),
            dma((4,)),
            dma((2 * REACH,)),
            dma((2 * REACH,)),
        ],
        compiler_params=pltpu.CompilerParams(
            collective_id=0, has_side_effects=True, vmem_limit_bytes=40 << 20
        ),
        name="cover",
    )(embeddings, cluster.reshape(-1, CHUNKS, CHUNK))
    return cover.reshape(rows), relative.reshape(rows)


def solution(mesh):
    placed = (P(("gx", "gy"), None), P())
    return jax.shard_map(
        per_device,
        mesh=mesh,
        in_specs=placed,
        out_specs=(P(("gx", "gy")), P(("gx", "gy"))),
        check_vma=False,
    )
```

time: 503 us -> 119 us (0.24)
  waiting for transfers between devices: 309 us -> 0 us
  Pallas kernels: 0 us -> 115 us
  blocking collectives: 79.3 us -> 0 us
  starting transfers between devices: 75.7 us -> 0 us
  matrix products: 22.8 us -> 0 us
  other arithmetic: 13.2 us -> 0 us
    ppermute x12 -> x0, waiting for transfers between devices: 309 us -> none  [passed_along(): return lax.ppermute(shard, axis, pairs)]
    pallas_call x0 -> x1, Pallas kernels: none -> 115 us  [per_device(): pl.pallas_call(kernel, out_shape=[jax.ShapeDtypeStruct((CHUNKS, CHUNK), j...]
    psum x1 -> x0, blocking collectives: 79.3 us -> none  [per_device(): lax.psum((local_sums, local_counts), ('gx', 'gy'))]
    ppermute x12 -> x0, starting transfers between devices: 75.7 us -> none  [passed_along(): return lax.ppermute(shard, axis, pairs)]
    dot_general x7 -> x0, matrix products: 22.8 us -> none  [the longest x5 20.9 us: tile_parts(): lax.dot_general(left_block, right_block, (((1,), (1,)), ((), ())), prefer...]
    reduce_sum x3 -> x0, other arithmetic: 10.5 us -> none  [the longest x1 8.02 us: tile_parts(): jnp.sum(jnp.where(is_live, jnp.exp(masked - row_max[:, None]), 0.0), axis=1)]
  transfers between devices with their start and end apart: 12 -> 0, of which waited for: 4 -> 0; matrix products, arithmetic and copies ran while one was open for 4% -> 0% of each run, Pallas kernels for 0% -> 0%
where the time goes in v1:
time: 119 us
  Pallas kernels  115 us (97%)
  local copies, waits for them, and re-layouts  4 us (3%)
    pallas_call x1, Pallas kernels, per_device(): pl.pallas_call(kernel, out_shape=[jax.ShapeDtypeStruct((CHUNKS, CHUNK), j...  115 us
    unnamed x6, local copies, waits for them, and re-layouts  4 us

profile of v1, /device:TPU:32, one launch (start us, length us, event | category | flops | bytes accessed | tf_op | source)
XLA Modules:
  0.0 119.2 jit_solution(10329961738431582363)
XLA Ops:
  0.6 0.0 copy-start
  0.6 1.6 %copy-done = bf16[1024,1024]{1,0:T(8,128)(2,1)S(1)} copy-done((bf16[1024,1024]{1,0:T(8,128)(2,1)S(1)}, bf16[1024,1024]{1,0:T(8,128)(2,1)}, u32[]{:S(2)}) %copy-start) | copy-done | bytes 2097176
  2.2 0.0 copy-start.1
  2.2 1.2 %copy-done.1 = s32[262144]{0:T(1024)S(1)} copy-done((s32[262144]{0:T(1024)S(1)}, s32[262144]{0:T(1024)}, u32[]{:S(2)}) %copy-start.1) | copy-done | bytes 1048600
  3.4 114.6 %cover.1 = (f32[8,128]{1,0:T(8,128)S(1)}, f32[8,128]{1,0:T(8,128)S(1)}) custom-call(bf16[1024,1024]{1,0:T(8,128)(2,1)S(1)} %copy-done, s32[256,8,128]{2,1,0:T(8,128)S(1)} %bitcast.3), custom_call_target="tpu_custom_call" | custom-call | tf_op jit(solution)/shard_map/cover/pallas_call | solution.py:294
  118.0 0.6 copy.6
  118.6 0.6 copy.7
Async XLA Ops:
  0.6 1.6 %copy-start = (bf16[1024,1024]{1,0:T(8,128)(2,1)S(1)}, bf16[1024,1024]{1,0:T(8,128)(2,1)}, u32[]{:S(2)}) copy-start(bf16[1024,1024]{1,0:T(8,128)(2,1)} %x_ref.1) | copy-start | bytes 6291460
  2.2 1.2 %copy-start.1 = (s32[262144]{0:T(1024)S(1)}, s32[262144]{0:T(1024)}, u32[]{:S(2)}) copy-start(s32[262144]{0:T(1024)} %param.3) | copy-start | bytes 3145732

commit v2 on v1

v2 whole, which is shorter than its diff:
```python
import math

import jax
import jax.numpy as jnp
from jax import lax
from jax.experimental import pallas as pl
from jax.experimental.pallas import tpu as pltpu
from jax.sharding import PartitionSpec as P

MESH = pl.DeviceIdType.MESH
INVERSE_TEMP = 100.0
EPSILON = 1e-06
SHIFT = 32.0
GAIN = INVERSE_TEMP * math.log2(math.e)
DROP = SHIFT * math.log2(math.e)

ROWS = 1024
CHUNK = 128
CHUNKS = ROWS // CHUNK
LEFT, RIGHT = 0, 1
REACH = 4
PERIOD = 16

S, C1, C2, C3, P1, P2, X = REACH, REACH + 1, REACH + 2, REACH + 3, REACH - 1, REACH - 2, 2 * REACH + 1
AWAY = 6
PART_OFFSETS = [-AWAY, -3, -2, -1, 1, 2, 3, AWAY]
COLUMNS = {S: 0, C1: 1, C2: 2, C3: 3, P1: 4, P2: 5}
DOWN = {C1: 0, C2: 1, C3: 2, P1: 3, P2: 4}
ACROSS = {S: 0, C1: 1, C2: 2, P1: 3, X: 4}


def chunk_rows(c):
    return pl.ds(pl.multiple_of(c * CHUNK, CHUNK), CHUNK)


def across(row):
    return jnp.transpose(jnp.broadcast_to(row, (CHUNK, CHUNK)))


def scores_of(left, right):
    return lax.dot_general(left, right, (((1,), (1,)), ((), ())), preferred_element_type=jnp.float32)


def each_chunk(body):
    def step(c, carry):
        body(c)
        return carry

    lax.fori_loop(0, CHUNKS, step, 0)


def kernel(
    x_ref, cluster_ref, cover_ref, relative_ref,
    raw, own, near, far, third, other, tags, columns, row_sums, col_sums, own_part, parts, parts_in, sums, sums_in,
    raw_sem, tags_sem, own_send, near_recv, relay_send, far_recv, relay2_send, third_recv, other_send, other_recv,
    parts_send, parts_recv, sums_send, sums_recv,
):
    gx, gy = lax.axis_index("gx"), lax.axis_index("gy")
    sizes = (lax.axis_size("gx"), lax.axis_size("gy"))
    devices = sizes[0] * sizes[1]
    me = gx * sizes[1] + gy

    d = lax.rem(me, PERIOD)
    leftward = (d >= 1) & (d <= 8)
    way = jnp.where(leftward, 1, -1)
    seat = jnp.where(leftward, d - 1, lax.rem(PERIOD - d, PERIOD))
    chain = jnp.where(leftward, RIGHT, LEFT)
    side = 1 - chain
    passes_own_back = (seat <= 2) | (seat == 7)
    has_c2 = seat <= 6
    has_c3 = seat <= 3
    has_p1 = seat <= 3
    first_seat = seat == 0
    passes_c2 = (seat >= 1) & (seat <= 4)
    lends_c2 = (seat >= 4) & (seat <= 6)
    has_other = (seat >= 1) & (seat <= 3)

    def block(offset):
        return lax.rem(me + (offset + devices), devices)

    def device(offset):
        place = block(offset)
        return (place // sizes[1], lax.rem(place, sizes[1]))

    other_core = (gx + 1 - 2 * lax.rem(gx, 2), gy)

    def raw_copy(c):
        return pltpu.make_async_copy(x_ref.at[chunk_rows(c)], raw.at[chunk_rows(c)], raw_sem.at[c])

    def tags_copy(k):
        offset = AWAY if k == X else k - REACH
        return pltpu.make_async_copy(cluster_ref.at[block(offset * way)], tags.at[k], tags_sem.at[k])

    def remote(src, dst, send_sem, recv_sem, to):
        return pltpu.make_async_remote_copy(
            src_ref=src, dst_ref=dst, send_sem=send_sem, recv_sem=recv_sem, device_id=to, device_id_type=MESH
        )

    def own_copy(which, c):
        rows = chunk_rows(c)
        return remote(
            own.at[rows], near.at[which, rows], own_send.at[which, c], near_recv.at[which, c], device(1 - 2 * which)
        )

    def relay_copy(which, c):
        rows = chunk_rows(c)
        return remote(
            near.at[which, rows], far.at[which, rows], relay_send.at[c], far_recv.at[which, c], device(1 - 2 * which)
        )

    def relay2_copy(which, c):
        rows = chunk_rows(c)
        return remote(
            far.at[which, rows], third.at[which, rows], relay2_send.at[c], third_recv.at[which, c], device(1 - 2 * which)
        )

    def other_copy(c):
        rows = chunk_rows(c)
        return remote(far.at[chain, rows], other.at[rows], other_send.at[c], other_recv.at[c], other_core)

    each_chunk(lambda c: raw_copy(c).start())
    for k in range(2 * REACH + 2):
        tags_copy(k).start()

    barrier = pltpu.get_barrier_semaphore()
    others = [k for k in range(-REACH, REACH + 1) if k != 0]
    met = [device(k) for k in others + [-AWAY, AWAY]] + [other_core]
    for to in met:
        pl.semaphore_signal(barrier, inc=1, device_id=to, device_id_type=MESH)

    def normalise(c):
        raw_copy(c).wait()

        def some(g, carry):
            rows = pl.ds(pl.multiple_of(c * CHUNK + g * 16, 16), 16)
            values = raw[rows].astype(jnp.float32)
            scale = lax.rsqrt(jnp.sum(values * values, axis=1, keepdims=True) + EPSILON)
            own[rows] = (values * scale).astype(jnp.bfloat16)
            return carry

        lax.fori_loop(0, CHUNK // 16, some, 0, unroll=2)

    def send_own(c):
        own_copy(chain, c).start()

        @pl.when(passes_own_back)
        def _():
            own_copy(side, c).start()

    normalise(0)
    pl.semaphore_wait(barrier, len(met))
    send_own(0)

    def send_step(c, carry):
        normalise(c)
        send_own(c)
        return carry

    lax.fori_loop(1, CHUNKS, send_step, 0)

    row_sums[...] = jnp.zeros_like(row_sums)
    col_sums[...] = jnp.zeros_like(col_sums)
    for k in range(2 * REACH + 2):
        tags_copy(k).wait()

    def columns_of(c):
        for kind, at in COLUMNS.items():
            columns[at, chunk_rows(c)] = across(tags[kind, pl.ds(c, 1), :])

    each_chunk(columns_of)

    refs = {S: own, C1: near.at[chain], C2: far.at[chain], C3: third.at[chain], P1: near.at[side], P2: far.at[side], X: other}

    def strip(down_kind, c, right_kind):
        down = refs[down_kind][chunk_rows(c)]
        down_tags = columns[COLUMNS[down_kind], chunk_rows(c)]
        same_block = down_kind == right_kind
        total = None
        for first in range(0, CHUNKS, 2):
            scores = scores_of(down, refs[right_kind][first * CHUNK : (first + 2) * CHUNK])
            for w in range(2):
                at = first + w
                live = down_tags == tags[right_kind, at : at + 1, :]
                if same_block:
                    place = lax.broadcasted_iota(jnp.int32, (CHUNK, CHUNK), 0) + (c - at) * CHUNK
                    live = live & (place != lax.broadcasted_iota(jnp.int32, (CHUNK, CHUNK), 1))
                cover = jnp.where(live, jnp.exp2(scores[:, w * CHUNK : (w + 1) * CHUNK] * GAIN - DROP), 0.0)
                total = cover if total is None else total + cover
                col_sums[ACROSS[right_kind], at] += jnp.sum(cover.reshape(CHUNK // 8, 8, CHUNK), axis=0)
        if not same_block:
            row_sums[DOWN[down_kind], chunk_rows(c)] += total

    each_chunk(lambda c: strip(S, c, S))

    def near_step(c):
        own_copy(chain, c).wait_recv()
        relay_copy(chain, c).start()

        @pl.when(d != 9)
        def _():
            strip(C1, c, S)

    each_chunk(near_step)

    @pl.when(has_c2)
    def _():
        def far_step(c):
            relay_copy(chain, c).wait_recv()

            @pl.when(passes_c2)
            def _():
                relay2_copy(chain, c).start()

            @pl.when(lends_c2)
            def _():
                other_copy(c).start()

            strip(C2, c, S)

        each_chunk(far_step)

    @pl.when(has_p1)
    def _():
        each_chunk(lambda c: own_copy(side, c).wait_recv())

        @pl.when(first_seat)
        def _():
            each_chunk(lambda c: strip(C1, c, P1))

        @pl.when(d == 1)
        def _():
            each_chunk(lambda c: strip(P1, c, S))

        each_chunk(lambda c: strip(C2, c, P1))

    @pl.when(has_other)
    def _():
        each_chunk(lambda c: other_copy(c).wait_recv())
        each_chunk(lambda c: strip(C2, c, X))

    @pl.when(has_c3)
    def _():
        def third_step(c):
            relay2_copy(chain, c).wait_recv()
            strip(C3, c, P1)

            @pl.when(seat == 3)
            def _():
                strip(C3, c, S)

            @pl.when(has_other & (d != 13))
            def _():
                strip(C3, c, X)

            @pl.when(first_seat)
            def _():
                relay_copy(side, c).wait_recv()
                strip(P2, c, C2)

                @pl.when(d == 1)
                def _():
                    strip(P2, c, C1)

        each_chunk(third_step)

    parts[...] = jnp.zeros_like(parts)
    for c in range(CHUNKS):
        rows = slice(c * CHUNK, (c + 1) * CHUNK)
        lane = slice(c, c + 1)
        for kind in (C1, C2, C3, P1, P2, X):
            total = None
            if kind in DOWN:
                total = jnp.sum(jnp.transpose(row_sums[DOWN[kind], rows]), axis=0, keepdims=True)
            if kind in ACROSS:
                more = jnp.sum(col_sums[ACROSS[kind], c], axis=0, keepdims=True)
                total = more if total is None else total + more
            at = PART_OFFSETS.index(AWAY if kind == X else kind - REACH)
            parts[jnp.where(leftward, at, len(PART_OFFSETS) - 1 - at), lane] = total
        own_part[lane] = jnp.sum(col_sums[ACROSS[S], c], axis=0, keepdims=True)

    def parts_copy(k):
        return remote(parts.at[k], parts_in.at[k], parts_send.at[k], parts_recv.at[k], device(PART_OFFSETS[k]))

    for k in range(len(PART_OFFSETS)):
        parts_copy(k).start()

    mine = tags[S]
    zero = jnp.zeros((CHUNKS, CHUNK), jnp.float32)

    def edge_tag(k):
        numbers = tags[REACH + k * way]
        at = numbers[CHUNKS - 1 : CHUNKS, CHUNK - 1 : CHUNK] if k < 0 else numbers[0:1, 0:1]
        return jnp.broadcast_to(at, (CHUNKS, CHUNK))

    def total_of(values):
        return jnp.broadcast_to(jnp.sum(values, keepdims=True), (CHUNKS, CHUNK))

    def own_totals(column_values):
        totals = []
        for j in range(CHUNKS):

            def add(c, acc):
                same = columns[COLUMNS[S], chunk_rows(c)] == tags[S, j : j + 1, :]
                picked = jnp.where(same, column_values(c), 0.0)
                return acc + jnp.sum(picked.reshape(CHUNK // 8, 8, CHUNK), axis=0)

            acc = lax.fori_loop(0, CHUNKS, add, jnp.zeros((8, CHUNK), jnp.float32), unroll=True)
            totals.append(jnp.sum(acc, axis=0, keepdims=True))
        return jnp.concatenate(totals, axis=0)

    counts = own_totals(lambda c: 1.0)
    for k in others:
        edge = edge_tag(k)
        many = total_of(jnp.where(tags[REACH + k * way] == edge, 1.0, 0.0))
        counts = counts + jnp.where(mine == edge, many, 0.0)

    total = own_part[...]
    for k in range(len(PART_OFFSETS)):
        parts_copy(k).wait_recv()
        total = total + parts_in[k]
    cover = jnp.where(
        total < math.exp(-SHIFT),
        jnp.log1p(jnp.minimum(total, math.exp(-SHIFT)) * math.exp(SHIFT)),
        SHIFT + jnp.log(total + math.exp(-SHIFT)),
    )
    cover_ref[...] = cover

    first_tag = jnp.broadcast_to(mine[0:1, 0:1], (CHUNKS, CHUNK))
    last_tag = jnp.broadcast_to(mine[CHUNKS - 1 : CHUNKS, CHUNK - 1 : CHUNK], (CHUNKS, CHUNK))
    sums[0] = total_of(jnp.where(mine == first_tag, cover, zero))
    sums[1] = total_of(jnp.where(mine == last_tag, cover, zero))

    def sums_copy(k):
        at = others.index(k)
        return remote(sums.at[0 if k < 0 else 1], sums_in.at[at], sums_send.at[at], sums_recv.at[at], device(k))

    for k in others:
        sums_copy(k).start()
    for c in range(CHUNKS):
        row_sums[0, c * CHUNK : (c + 1) * CHUNK] = across(cover[c : c + 1])
    cluster_sums = own_totals(lambda c: row_sums[0, chunk_rows(c)])
    for k in others:
        sums_copy(k).wait_recv()
        cluster_sums = cluster_sums + jnp.where(mine == edge_tag(-k), sums_in[others.index(k)], zero)
    relative_ref[...] = cover - cluster_sums / counts

    def sent(c):
        own_copy(chain, c).wait_send()
        relay_copy(chain, c).wait_send()

        @pl.when(passes_own_back)
        def _():
            own_copy(side, c).wait_send()

        @pl.when(passes_c2)
        def _():
            relay2_copy(chain, c).wait_send()

        @pl.when(lends_c2)
        def _():
            other_copy(c).wait_send()

    each_chunk(sent)
    for k in range(len(PART_OFFSETS)):
        parts_copy(k).wait_send()
    for k in others:
        sums_copy(k).wait_send()


def per_device(embeddings, cluster):
    rows, width = embeddings.shape
    vmem = pl.BlockSpec(memory_space=pltpu.VMEM)
    hbm = pl.BlockSpec(memory_space=pltpu.HBM)
    dma = pltpu.SemaphoreType.DMA
    small = (CHUNKS, CHUNK)
    cover, relative = pl.pallas_call(
        kernel,
        out_shape=[jax.ShapeDtypeStruct(small, jnp.float32)] * 2,
        in_specs=[hbm, hbm],
        out_specs=[vmem, vmem],
        scratch_shapes=[
            pltpu.VMEM((rows, width), jnp.bfloat16),
            pltpu.VMEM((rows, width), jnp.bfloat16),
            pltpu.VMEM((2, rows, width), jnp.bfloat16),
            pltpu.VMEM((2, rows, width), jnp.bfloat16),
            pltpu.VMEM((2, rows, width), jnp.bfloat16),
            pltpu.VMEM((rows, width), jnp.bfloat16),
            pltpu.VMEM((2 * REACH + 2, *small), jnp.int32),
            pltpu.VMEM((len(COLUMNS), rows, CHUNK), jnp.int32),
            pltpu.VMEM((len(DOWN), rows, CHUNK), jnp.float32),
            pltpu.VMEM((len(ACROSS), CHUNKS, 8, CHUNK), jnp.float32),
            pltpu.VMEM(small, jnp.float32),
            pltpu.VMEM((len(PART_OFFSETS), *small), jnp.float32),
            pltpu.VMEM((len(PART_OFFSETS), *small), jnp.float32),
            pltpu.VMEM((2, *small), jnp.float32),
            pltpu.VMEM((2 * REACH, *small), jnp.float32),
            dma((CHUNKS,)),
            dma((2 * REACH + 2,)),
            dma((2, CHUNKS)),
            dma((2, CHUNKS)),
            dma((CHUNKS,)),
            dma((2, CHUNKS)),
            dma((CHUNKS,)),
            dma((2, CHUNKS)),
            dma((CHUNKS,)),
            dma((CHUNKS,)),
            dma((len(PART_OFFSETS),)),
            dma((len(PART_OFFSETS),)),
            dma((2 * REACH,)),
            dma((2 * REACH,)),
        ],
        compiler_params=pltpu.CompilerParams(
            collective_id=0, has_side_effects=True, vmem_limit_bytes=60 << 20
        ),
        name="cover",
    )(embeddings, cluster.reshape(-1, *small))
    return cover.reshape(rows), relative.reshape(rows)


def solution(mesh):
    placed = (P(("gx", "gy"), None), P())
    return jax.shard_map(
        per_device,
        mesh=mesh,
        in_specs=placed,
        out_specs=(P(("gx", "gy")), P(("gx", "gy"))),
        check_vma=False,
    )
```

time: 119 us -> 123 us (1.034)
  Pallas kernels: 115 us -> 119 us
  local copies, waits for them, and re-layouts: 4 us -> 2.53 us
    pallas_call x1, Pallas kernels: 115 us -> 119 us  [per_device(): pl.pallas_call(kernel, out_shape=[jax.ShapeDtypeStruct(small, jnp.float32...]
    unnamed x6 -> x2, local copies, waits for them, and re-layouts: 4 us -> 2.53 us
where the time goes in v2:
time: 123 us; the launch traced here: 122 us
  Pallas kernels  119 us (97%)
  local copies, waits for them, and re-layouts  2.53 us (2%)
    pallas_call x1, Pallas kernels, per_device(): pl.pallas_call(kernel, out_shape=[jax.ShapeDtypeStruct(small, jnp.float32...  119 us
    unnamed x2, local copies, waits for them, and re-layouts  2.53 us

profile of v2, /device:TPU:32, one launch (start us, length us, event | category | flops | bytes accessed | tf_op | source)
XLA Modules:
  0.0 122.4 jit_solution(4411932598961664631)
XLA Ops:
  0.6 119.3 %cover.1 = (f32[8,128]{1,0:T(8,128)}, f32[8,128]{1,0:T(8,128)}) custom-call(bf16[1024,1024]{1,0:T(8,128)(2,1)} %x_ref.1, s32[256,8,128]{2,1,0:T(8,128)} %bitcast.3), custom_call_target="tpu_custom_call" | custom-call | tf_op jit(solution)/shard_map/cover/pallas_call | solution.py:376
  119.9 1.3 %copy.6 = f32[1024]{0:T(1024)} copy(f32[1024]{0:T(1024)} %bitcast.5) | data formatting | bytes 8192
  121.2 1.3 %copy.7 = f32[1024]{0:T(1024)} copy(f32[1024]{0:T(1024)} %bitcast.4) | data formatting | bytes 8192

commit v3 on v2

--- a/solution.py
+++ b/solution.py
@@ -24,13 +24,18 @@
 S, C1, C2, C3, P1, P2, X = REACH, REACH + 1, REACH + 2, REACH + 3, REACH - 1, REACH - 2, 2 * REACH + 1
 AWAY = 6
 PART_OFFSETS = [-AWAY, -3, -2, -1, 1, 2, 3, AWAY]
-COLUMNS = {S: 0, C1: 1, C2: 2, C3: 3, P1: 4, P2: 5}
-DOWN = {C1: 0, C2: 1, C3: 2, P1: 3, P2: 4}
-ACROSS = {S: 0, C1: 1, C2: 2, P1: 3, X: 4}
+PAIR = 2 * CHUNK
+PAIRS = ROWS // PAIR
+DOWN = {S: 0, C1: 1, C2: 2, P1: 3, X: 4}
+ACROSS = {S: 0, C1: 1, C2: 2, C3: 3, P1: 4, P2: 5, X: 6}
 
 
 def chunk_rows(c):
     return pl.ds(pl.multiple_of(c * CHUNK, CHUNK), CHUNK)
+
+
+def pair_rows(c):
+    return pl.ds(pl.multiple_of(c * PAIR, PAIR), PAIR)
 
 
 def across(row):
@@ -47,6 +52,14 @@
         return carry
 
     lax.fori_loop(0, CHUNKS, step, 0)
+
+
+def each_pair(body):
+    def step(c, carry):
+        body(c)
+        return carry
+
+    lax.fori_loop(0, PAIRS, step, 0)
 
 
 def kernel(
@@ -82,6 +95,12 @@
         place = block(offset)
         return (place // sizes[1], lax.rem(place, sizes[1]))
 
+    def chunk(n):
+        return jnp.where(leftward, n, CHUNKS - 1 - n)
+
+    def pair(n):
+        return jnp.where(leftward, n, PAIRS - 1 - n)
+
     other_core = (gx + 1 - 2 * lax.rem(gx, 2), gy)
 
     def raw_copy(c):
@@ -118,7 +137,7 @@
         rows = chunk_rows(c)
         return remote(far.at[chain, rows], other.at[rows], other_send.at[c], other_recv.at[c], other_core)
 
-    each_chunk(lambda c: raw_copy(c).start())
+    each_chunk(lambda n: raw_copy(chunk(n)).start())
     for k in range(2 * REACH + 2):
         tags_copy(k).start()
 
@@ -143,20 +162,24 @@
     def send_own(c):
         own_copy(chain, c).start()
 
-        @pl.when(passes_own_back)
+        @pl.when(seat <= 2)
         def _():
             own_copy(side, c).start()
 
-    normalise(0)
+    normalise(chunk(0))
     pl.semaphore_wait(barrier, len(met))
-    send_own(0)
-
-    def send_step(c, carry):
-        normalise(c)
-        send_own(c)
+    send_own(chunk(0))
+
+    def send_step(n, carry):
+        normalise(chunk(n))
+        send_own(chunk(n))
         return carry
 
     lax.fori_loop(1, CHUNKS, send_step, 0)
+
+    @pl.when(seat == 7)
+    def _():
+        each_chunk(lambda n: own_copy(side, chunk(CHUNKS - 1 - n)).start())
 
     row_sums[...] = jnp.zeros_like(row_sums)
     col_sums[...] = jnp.zeros_like(col_sums)
@@ -164,60 +187,81 @@
         tags_copy(k).wait()
 
     def columns_of(c):
-        for kind, at in COLUMNS.items():
+        for kind, at in DOWN.items():
             columns[at, chunk_rows(c)] = across(tags[kind, pl.ds(c, 1), :])
 
     each_chunk(columns_of)
 
     refs = {S: own, C1: near.at[chain], C2: far.at[chain], C3: third.at[chain], P1: near.at[side], P2: far.at[side], X: other}
 
-    def strip(down_kind, c, right_kind):
-        down = refs[down_kind][chunk_rows(c)]
-        down_tags = columns[COLUMNS[down_kind], chunk_rows(c)]
-        same_block = down_kind == right_kind
-        total = None
-        for first in range(0, CHUNKS, 2):
-            scores = scores_of(down, refs[right_kind][first * CHUNK : (first + 2) * CHUNK])
+    def strip(arrived, c, resident, after=None):
+        late = refs[arrived][pair_rows(c)]
+        same_block = arrived == resident
+
+        def part(rows, size):
+            scores = scores_of(refs[resident][rows], late)
+            numbers = columns[DOWN[resident], rows]
+            total = None
             for w in range(2):
-                at = first + w
-                live = down_tags == tags[right_kind, at : at + 1, :]
+                at = pl.ds(2 * c + w, 1)
+                live = numbers == tags[arrived, at, :]
                 if same_block:
-                    place = lax.broadcasted_iota(jnp.int32, (CHUNK, CHUNK), 0) + (c - at) * CHUNK
-                    live = live & (place != lax.broadcasted_iota(jnp.int32, (CHUNK, CHUNK), 1))
+                    place = lax.broadcasted_iota(jnp.int32, (size, CHUNK), 0) - (2 * c + w) * CHUNK
+                    live = live & (place != lax.broadcasted_iota(jnp.int32, (size, CHUNK), 1))
                 cover = jnp.where(live, jnp.exp2(scores[:, w * CHUNK : (w + 1) * CHUNK] * GAIN - DROP), 0.0)
                 total = cover if total is None else total + cover
-                col_sums[ACROSS[right_kind], at] += jnp.sum(cover.reshape(CHUNK // 8, 8, CHUNK), axis=0)
-        if not same_block:
-            row_sums[DOWN[down_kind], chunk_rows(c)] += total
-
-    each_chunk(lambda c: strip(S, c, S))
-
-    def near_step(c):
-        own_copy(chain, c).wait_recv()
-        relay_copy(chain, c).start()
+                col_sums[ACROSS[arrived], at] += jnp.sum(cover.reshape(size // 8, 8, CHUNK), axis=0)[None]
+            if not same_block:
+                row_sums[DOWN[resident], rows] += total
+
+        if after is None:
+            part(pl.ds(0, ROWS), ROWS)
+        else:
+            first, place_of = after
+
+            def some(j, carry):
+                part(pair_rows(place_of(j)), PAIR)
+                return carry
+
+            lax.fori_loop(first, PAIRS, some, 0)
+
+    each_pair(lambda c: strip(S, c, S))
+
+    def near_step(n):
+        for h in range(2):
+            c = chunk(2 * n + h)
+            own_copy(chain, c).wait_recv()
+            relay_copy(chain, c).start()
 
         @pl.when(d != 9)
         def _():
-            strip(C1, c, S)
-
-    each_chunk(near_step)
+            strip(C1, pair(n), S)
+
+    each_pair(near_step)
 
     @pl.when(has_c2)
     def _():
-        def far_step(c):
-            relay_copy(chain, c).wait_recv()
-
-            @pl.when(passes_c2)
-            def _():
-                relay2_copy(chain, c).start()
-
-            @pl.when(lends_c2)
-            def _():
-                other_copy(c).start()
-
-            strip(C2, c, S)
-
-        each_chunk(far_step)
+        def far_step(n):
+            for h in range(2):
+                c = chunk(2 * n + h)
+                relay_copy(chain, c).wait_recv()
+
+                @pl.when(passes_c2)
+                def _():
+                    relay2_copy(chain, c).start()
+
+                @pl.when(lends_c2)
+                def _():
+                    other_copy(c).start()
+
+            strip(C2, pair(n), S)
+
+        each_pair(far_step)
+
+    @pl.when(has_other)
+    def _():
+        each_chunk(lambda c: other_copy(c).wait_recv())
+        each_pair(lambda n: strip(X, pair(n), C2, (n, pair)))
 
     @pl.when(has_p1)
     def _():
@@ -225,58 +269,60 @@
 
         @pl.when(first_seat)
         def _():
-            each_chunk(lambda c: strip(C1, c, P1))
+            each_pair(lambda c: strip(C1, c, P1))
 
         @pl.when(d == 1)
         def _():
-            each_chunk(lambda c: strip(P1, c, S))
-
-        each_chunk(lambda c: strip(C2, c, P1))
-
-    @pl.when(has_other)
-    def _():
-        each_chunk(lambda c: other_copy(c).wait_recv())
-        each_chunk(lambda c: strip(C2, c, X))
+            each_pair(lambda c: strip(P1, c, S))
+
+        each_pair(lambda c: strip(C2, c, P1))
 
     @pl.when(has_c3)
     def _():
-        def third_step(c):
-            relay2_copy(chain, c).wait_recv()
-            strip(C3, c, P1)
+        def third_step(n):
+            for h in range(2):
+                relay2_copy(chain, chunk(2 * n + h)).wait_recv()
+            strip(C3, pair(n), P1, (n, pair))
 
             @pl.when(seat == 3)
             def _():
-                strip(C3, c, S)
+                strip(C3, pair(n), S)
 
             @pl.when(has_other & (d != 13))
             def _():
-                strip(C3, c, X)
+                strip(C3, pair(n), X)
 
             @pl.when(first_seat)
             def _():
-                relay_copy(side, c).wait_recv()
-                strip(P2, c, C2)
+                for h in range(2):
+                    relay_copy(side, chunk(CHUNKS - 1 - 2 * n - h)).wait_recv()
+                strip(P2, pair(PAIRS - 1 - n), C2, (n, lambda j: pair(PAIRS - 1 - j)))
 
                 @pl.when(d == 1)
                 def _():
-                    strip(P2, c, C1)
-
-        each_chunk(third_step)
+                    strip(P2, pair(PAIRS - 1 - n), C1)
+
+        each_pair(third_step)
+
+    ones = jnp.ones((8, CHUNK), jnp.float32)
+
+    def sums_of(kind):
+        total = None
+        if kind in ACROSS:
+            total = jnp.sum(col_sums[ACROSS[kind]], axis=1)
+        if kind in DOWN:
+            rows = lax.dot_general(
+                ones, row_sums[DOWN[kind]], (((1,), (1,)), ((), ())),
+                precision=lax.Precision.HIGHEST, preferred_element_type=jnp.float32,
+            )
+            total = total + jnp.concatenate([rows[0:1, c * CHUNK : (c + 1) * CHUNK] for c in range(CHUNKS)], axis=0)
+        return total
 
     parts[...] = jnp.zeros_like(parts)
-    for c in range(CHUNKS):
-        rows = slice(c * CHUNK, (c + 1) * CHUNK)
-        lane = slice(c, c + 1)
-        for kind in (C1, C2, C3, P1, P2, X):
-            total = None
-            if kind in DOWN:
-                total = jnp.sum(jnp.transpose(row_sums[DOWN[kind], rows]), axis=0, keepdims=True)
-            if kind in ACROSS:
-                more = jnp.sum(col_sums[ACROSS[kind], c], axis=0, keepdims=True)
-                total = more if total is None else total + more
-            at = PART_OFFSETS.index(AWAY if kind == X else kind - REACH)
-            parts[jnp.where(leftward, at, len(PART_OFFSETS) - 1 - at), lane] = total
-        own_part[lane] = jnp.sum(col_sums[ACROSS[S], c], axis=0, keepdims=True)
+    for kind in (C1, C2, C3, P1, P2, X):
+        at = PART_OFFSETS.index(AWAY if kind == X else kind - REACH)
+        parts[jnp.where(leftward, at, len(PART_OFFSETS) - 1 - at)] = sums_of(kind)
+    own_part[...] = sums_of(S)
 
     def parts_copy(k):
         return remote(parts.at[k], parts_in.at[k], parts_send.at[k], parts_recv.at[k], device(PART_OFFSETS[k]))
@@ -300,7 +346,7 @@
         for j in range(CHUNKS):
 
             def add(c, acc):
-                same = columns[COLUMNS[S], chunk_rows(c)] == tags[S, j : j + 1, :]
+                same = columns[DOWN[S], chunk_rows(c)] == tags[S, j : j + 1, :]
                 picked = jnp.where(same, column_values(c), 0.0)
                 return acc + jnp.sum(picked.reshape(CHUNK // 8, 8, CHUNK), axis=0)
 
@@ -386,7 +432,7 @@
             pltpu.VMEM((2, rows, width), jnp.bfloat16),
             pltpu.VMEM((rows, width), jnp.bfloat16),
             pltpu.VMEM((2 * REACH + 2, *small), jnp.int32),
-            pltpu.VMEM((len(COLUMNS), rows, CHUNK), jnp.int32),
+            pltpu.VMEM((len(DOWN), rows, CHUNK), jnp.int32),
             pltpu.VMEM((len(DOWN), rows, CHUNK), jnp.float32),
             pltpu.VMEM((len(ACROSS), CHUNKS, 8, CHUNK), jnp.float32),
             pltpu.VMEM(small, jnp.float32),

time: 123 us -> 113 us (0.919)
  Pallas kernels: 119 us -> 109 us
    pallas_call x1, Pallas kernels: 119 us -> 109 us  [per_device(): pl.pallas_call(kernel, out_shape=[jax.ShapeDtypeStruct(small, jnp.float32...]
where the time goes in v3:
time: 113 us; the launch traced here: 112 us
  Pallas kernels  109 us (96%)
  local copies, waits for them, and re-layouts  2.53 us (2%)
    pallas_call x1, Pallas kernels, per_device(): pl.pallas_call(kernel, out_shape=[jax.ShapeDtypeStruct(small, jnp.float32...  109 us
    unnamed x2, local copies, waits for them, and re-layouts  2.53 us

profile of v3, /device:TPU:32, one launch (start us, length us, event | category | flops | bytes accessed | tf_op | source)
XLA Modules:
  0.0 112.1 jit_solution(9074186183286641691)
XLA Ops:
  0.6 108.9 %cover.1 = (f32[8,128]{1,0:T(8,128)}, f32[8,128]{1,0:T(8,128)}) custom-call(bf16[1024,1024]{1,0:T(8,128)(2,1)} %x_ref.1, s32[256,8,128]{2,1,0:T(8,128)} %bitcast.3), custom_call_target="tpu_custom_call" | custom-call | tf_op jit(solution)/shard_map/cover/pallas_call | solution.py:422
  109.5 1.3 %copy.6 = f32[1024]{0:T(1024)} copy(f32[1024]{0:T(1024)} %bitcast.5) | data formatting | bytes 8192
  110.8 1.3 %copy.7 = f32[1024]{0:T(1024)} copy(f32[1024]{0:T(1024)} %bitcast.4) | data formatting | bytes 8192

commit v4 on v3

--- a/solution.py
+++ b/solution.py
@@ -64,7 +64,7 @@
 
 def kernel(
     x_ref, cluster_ref, cover_ref, relative_ref,
-    raw, own, near, far, third, other, tags, columns, row_sums, col_sums, own_part, parts, parts_in, sums, sums_in,
+    raw, own, near, far, third, other, tags, columns, row_sums, col_sums, row_counts, own_part, parts, parts_in, sums, sums_in,
     raw_sem, tags_sem, own_send, near_recv, relay_send, far_recv, relay2_send, third_recv, other_send, other_recv,
     parts_send, parts_recv, sums_send, sums_recv,
 ):
@@ -160,11 +160,13 @@
         lax.fori_loop(0, CHUNK // 16, some, 0, unroll=2)
 
     def send_own(c):
-        own_copy(chain, c).start()
-
-        @pl.when(seat <= 2)
+        @pl.when(seat != 0)
         def _():
-            own_copy(side, c).start()
+            own_copy(chain, c).start()
+
+    def send_late(n):
+        for h in range(2):
+            own_copy(side, chunk(CHUNKS - 1 - 2 * n - h)).start()
 
     normalise(chunk(0))
     pl.semaphore_wait(barrier, len(met))
@@ -179,7 +181,7 @@
 
     @pl.when(seat == 7)
     def _():
-        each_chunk(lambda n: own_copy(side, chunk(CHUNKS - 1 - n)).start())
+        each_pair(send_late)
 
     row_sums[...] = jnp.zeros_like(row_sums)
     col_sums[...] = jnp.zeros_like(col_sums)
@@ -192,38 +194,64 @@
 
     each_chunk(columns_of)
 
+    mine = tags[S]
+    zero = jnp.zeros((CHUNKS, CHUNK), jnp.float32)
+
+    def edge_tag(k):
+        numbers = tags[REACH + k * way]
+        at = numbers[CHUNKS - 1 : CHUNKS, CHUNK - 1 : CHUNK] if k < 0 else numbers[0:1, 0:1]
+        return jnp.broadcast_to(at, (CHUNKS, CHUNK))
+
+    def total_of(values):
+        return jnp.broadcast_to(jnp.sum(values, keepdims=True), (CHUNKS, CHUNK))
+
+    def own_totals(column_values):
+        totals = []
+        for j in range(CHUNKS):
+
+            def add(c, acc):
+                same = columns[DOWN[S], chunk_rows(c)] == tags[S, j : j + 1, :]
+                picked = jnp.where(same, column_values(c), 0.0)
+                return acc + jnp.sum(picked.reshape(CHUNK // 8, 8, CHUNK), axis=0)
+
+            acc = lax.fori_loop(0, CHUNKS, add, jnp.zeros((8, CHUNK), jnp.float32), unroll=True)
+            totals.append(jnp.sum(acc, axis=0, keepdims=True))
+        return jnp.concatenate(totals, axis=0)
+
+    counts = own_totals(lambda c: 1.0)
+    for k in others:
+        edge = edge_tag(k)
+        many = total_of(jnp.where(tags[REACH + k * way] == edge, 1.0, 0.0))
+        counts = counts + jnp.where(mine == edge, many, 0.0)
+    row_counts[...] = counts
+
     refs = {S: own, C1: near.at[chain], C2: far.at[chain], C3: third.at[chain], P1: near.at[side], P2: far.at[side], X: other}
 
-    def strip(arrived, c, resident, after=None):
-        late = refs[arrived][pair_rows(c)]
-        same_block = arrived == resident
-
-        def part(rows, size):
-            scores = scores_of(refs[resident][rows], late)
-            numbers = columns[DOWN[resident], rows]
-            total = None
-            for w in range(2):
-                at = pl.ds(2 * c + w, 1)
-                live = numbers == tags[arrived, at, :]
-                if same_block:
-                    place = lax.broadcasted_iota(jnp.int32, (size, CHUNK), 0) - (2 * c + w) * CHUNK
-                    live = live & (place != lax.broadcasted_iota(jnp.int32, (size, CHUNK), 1))
-                cover = jnp.where(live, jnp.exp2(scores[:, w * CHUNK : (w + 1) * CHUNK] * GAIN - DROP), 0.0)
-                total = cover if total is None else total + cover
-                col_sums[ACROSS[arrived], at] += jnp.sum(cover.reshape(size // 8, 8, CHUNK), axis=0)[None]
-            if not same_block:
-                row_sums[DOWN[resident], rows] += total
-
-        if after is None:
-            part(pl.ds(0, ROWS), ROWS)
-        else:
-            first, place_of = after
-
-            def some(j, carry):
-                part(pair_rows(place_of(j)), PAIR)
-                return carry
-
-            lax.fori_loop(first, PAIRS, some, 0)
+    def piece(arrived, c, resident, rows, size):
+        scores = scores_of(refs[resident][rows], refs[arrived][pair_rows(c)])
+        numbers = columns[DOWN[resident], rows]
+        total = None
+        for w in range(2):
+            at = pl.ds(2 * c + w, 1)
+            live = numbers == tags[arrived, at, :]
+            if arrived == resident:
+                place = lax.broadcasted_iota(jnp.int32, (size, CHUNK), 0) - (2 * c + w) * CHUNK
+                live = live & (place != lax.broadcasted_iota(jnp.int32, (size, CHUNK), 1))
+            cover = jnp.where(live, jnp.exp2(scores[:, w * CHUNK : (w + 1) * CHUNK] * GAIN - DROP), 0.0)
+            total = cover if total is None else total + cover
+            col_sums[ACROSS[arrived], at] += jnp.sum(cover.reshape(size // 8, 8, CHUNK), axis=0)[None]
+        if arrived != resident:
+            row_sums[DOWN[resident], rows] += total
+
+    def strip(arrived, c, resident):
+        piece(arrived, c, resident, pl.ds(0, ROWS), ROWS)
+
+    def pieces(first, last, arrived, c_of, resident, r_of):
+        def some(j, carry):
+            piece(arrived, c_of(j), resident, pair_rows(r_of(j)), PAIR)
+            return carry
+
+        lax.fori_loop(first, last, some, 0)
 
     each_pair(lambda c: strip(S, c, S))
 
@@ -233,6 +261,10 @@
             own_copy(chain, c).wait_recv()
             relay_copy(chain, c).start()
 
+            @pl.when(seat == 0)
+            def _():
+                own_copy(chain, c).start()
+
         @pl.when(d != 9)
         def _():
             strip(C1, pair(n), S)
@@ -254,35 +286,53 @@
                 def _():
                     other_copy(c).start()
 
+            @pl.when((seat <= 2) & (n >= 2))
+            def _():
+                send_late(n - 2)
+
             strip(C2, pair(n), S)
 
         each_pair(far_step)
 
+    @pl.when(seat <= 2)
+    def _():
+        send_late(2)
+        send_late(3)
+
     @pl.when(has_other)
     def _():
-        each_chunk(lambda c: other_copy(c).wait_recv())
-        each_pair(lambda n: strip(X, pair(n), C2, (n, pair)))
-
-    @pl.when(has_p1)
-    def _():
-        each_chunk(lambda c: own_copy(side, c).wait_recv())
-
-        @pl.when(first_seat)
-        def _():
-            each_pair(lambda c: strip(C1, c, P1))
-
-        @pl.when(d == 1)
-        def _():
-            each_pair(lambda c: strip(P1, c, S))
-
-        each_pair(lambda c: strip(C2, c, P1))
+        def other_step(n):
+            last = PAIRS - 1 - n
+            for h in range(2):
+                other_copy(chunk(2 * last + 1 - h)).wait_recv()
+            pieces(last, PAIRS, X, lambda j: pair(last), C2, pair)
+
+        each_pair(other_step)
+
+    def side_step(n):
+        last = PAIRS - 1 - n
+        for h in range(2):
+            own_copy(side, chunk(2 * last + 1 - h)).wait_recv()
+        strip(P1, pair(last), C2)
+
+    @pl.when(first_seat)
+    def _():
+        def first_step(n):
+            side_step(n)
+            strip(P1, pair(PAIRS - 1 - n), C1)
+
+            @pl.when(d == 1)
+            def _():
+                strip(P1, pair(PAIRS - 1 - n), S)
+
+        each_pair(first_step)
 
     @pl.when(has_c3)
     def _():
         def third_step(n):
+            last = PAIRS - 1 - n
             for h in range(2):
                 relay2_copy(chain, chunk(2 * n + h)).wait_recv()
-            strip(C3, pair(n), P1, (n, pair))
 
             @pl.when(seat == 3)
             def _():
@@ -292,30 +342,32 @@
             def _():
                 strip(C3, pair(n), X)
 
+            @pl.when(has_other)
+            def _():
+                side_step(n)
+
+            pieces(jnp.maximum(n, last), PAIRS, C3, lambda j: pair(n), P1, pair)
+            pieces(0, jnp.minimum(n, last + 1), C3, pair, P1, lambda j: pair(last))
+
             @pl.when(first_seat)
             def _():
                 for h in range(2):
-                    relay_copy(side, chunk(CHUNKS - 1 - 2 * n - h)).wait_recv()
-                strip(P2, pair(PAIRS - 1 - n), C2, (n, lambda j: pair(PAIRS - 1 - j)))
+                    relay_copy(side, chunk(2 * last + 1 - h)).wait_recv()
+                pieces(n, PAIRS, P2, lambda j: pair(last), C2, lambda j: pair(PAIRS - 1 - j))
 
                 @pl.when(d == 1)
                 def _():
-                    strip(P2, pair(PAIRS - 1 - n), C1)
+                    strip(P2, pair(last), C1)
 
         each_pair(third_step)
-
-    ones = jnp.ones((8, CHUNK), jnp.float32)
 
     def sums_of(kind):
         total = None
         if kind in ACROSS:
             total = jnp.sum(col_sums[ACROSS[kind]], axis=1)
         if kind in DOWN:
-            rows = lax.dot_general(
-                ones, row_sums[DOWN[kind]], (((1,), (1,)), ((), ())),
-                precision=lax.Precision.HIGHEST, preferred_element_type=jnp.float32,
-            )
-            total = total + jnp.concatenate([rows[0:1, c * CHUNK : (c + 1) * CHUNK] for c in range(CHUNKS)], axis=0)
+            rows = [row_sums[DOWN[kind], c * CHUNK : (c + 1) * CHUNK] for c in range(CHUNKS)]
+            total = total + jnp.concatenate([jnp.sum(jnp.transpose(r), axis=0, keepdims=True) for r in rows], axis=0)
         return total
 
     parts[...] = jnp.zeros_like(parts)
@@ -329,36 +381,6 @@
 
     for k in range(len(PART_OFFSETS)):
         parts_copy(k).start()
-
-    mine = tags[S]
-    zero = jnp.zeros((CHUNKS, CHUNK), jnp.float32)
-
-    def edge_tag(k):
-        numbers = tags[REACH + k * way]
-        at = numbers[CHUNKS - 1 : CHUNKS, CHUNK - 1 : CHUNK] if k < 0 else numbers[0:1, 0:1]
-        return jnp.broadcast_to(at, (CHUNKS, CHUNK))
-
-    def total_of(values):
-        return jnp.broadcast_to(jnp.sum(values, keepdims=True), (CHUNKS, CHUNK))
-
-    def own_totals(column_values):
-        totals = []
-        for j in range(CHUNKS):
-
-            def add(c, acc):
-                same = columns[DOWN[S], chunk_rows(c)] == tags[S, j : j + 1, :]
-                picked = jnp.where(same, column_values(c), 0.0)
-                return acc + jnp.sum(picked.reshape(CHUNK // 8, 8, CHUNK), axis=0)
-
-            acc = lax.fori_loop(0, CHUNKS, add, jnp.zeros((8, CHUNK), jnp.float32), unroll=True)
-            totals.append(jnp.sum(acc, axis=0, keepdims=True))
-        return jnp.concatenate(totals, axis=0)
-
-    counts = own_totals(lambda c: 1.0)
-    for k in others:
-        edge = edge_tag(k)
-        many = total_of(jnp.where(tags[REACH + k * way] == edge, 1.0, 0.0))
-        counts = counts + jnp.where(mine == edge, many, 0.0)
 
     total = own_part[...]
     for k in range(len(PART_OFFSETS)):
@@ -388,7 +410,7 @@
     for k in others:
         sums_copy(k).wait_recv()
         cluster_sums = cluster_sums + jnp.where(mine == edge_tag(-k), sums_in[others.index(k)], zero)
-    relative_ref[...] = cover - cluster_sums / counts
+    relative_ref[...] = cover - cluster_sums / row_counts[...]
 
     def sent(c):
         own_copy(chain, c).wait_send()
@@ -435,6 +457,7 @@
             pltpu.VMEM((len(DOWN), rows, CHUNK), jnp.int32),
             pltpu.VMEM((len(DOWN), rows, CHUNK), jnp.float32),
             pltpu.VMEM((len(ACROSS), CHUNKS, 8, CHUNK), jnp.float32),
+            pltpu.VMEM(small, jnp.float32),
             pltpu.VMEM(small, jnp.float32),
             pltpu.VMEM((len(PART_OFFSETS), *small), jnp.float32),
             pltpu.VMEM((len(PART_OFFSETS), *small), jnp.float32),

time: 113 us -> 110 us (0.973)
  Pallas kernels: 109 us -> 107 us
    pallas_call x1, Pallas kernels: 109 us -> 107 us  [per_device(): pl.pallas_call(kernel, out_shape=[jax.ShapeDtypeStruct(small, jnp.float32...]
where the time goes in v4:
time: 110 us
  Pallas kernels  107 us (97%)
  local copies, waits for them, and re-layouts  2.53 us (2%)
    pallas_call x1, Pallas kernels, per_device(): pl.pallas_call(kernel, out_shape=[jax.ShapeDtypeStruct(small, jnp.float32...  107 us
    unnamed x2, local copies, waits for them, and re-layouts  2.53 us

profile of v4, /device:TPU:32, one launch (start us, length us, event | category | flops | bytes accessed | tf_op | source)
XLA Modules:
  0.0 110.0 jit_solution(6071906640299243940)
XLA Ops:
  0.6 106.8 %cover.1 = (f32[8,128]{1,0:T(8,128)}, f32[8,128]{1,0:T(8,128)}) custom-call(bf16[1024,1024]{1,0:T(8,128)(2,1)} %x_ref.1, s32[256,8,128]{2,1,0:T(8,128)} %bitcast.3), custom_call_target="tpu_custom_call" | custom-call | tf_op jit(solution)/shard_map/cover/pallas_call | solution.py:444
  107.5 1.3 %copy.6 = f32[1024]{0:T(1024)} copy(f32[1024]{0:T(1024)} %bitcast.5) | data formatting | bytes 8192
  108.7 1.3 %copy.7 = f32[1024]{0:T(1024)} copy(f32[1024]{0:T(1024)} %bitcast.4) | data formatting | bytes 8192

commit v5 on v4

--- a/solution.py
+++ b/solution.py
@@ -64,7 +64,7 @@
 
 def kernel(
     x_ref, cluster_ref, cover_ref, relative_ref,
-    raw, own, near, far, third, other, tags, columns, row_sums, col_sums, row_counts, own_part, parts, parts_in, sums, sums_in,
+    raw, own, near, far, third, other, tags, columns, row_sums, col_sums, row_counts, masks, own_part, parts, parts_in, sums, sums_in,
     raw_sem, tags_sem, own_send, near_recv, relay_send, far_recv, relay2_send, third_recv, other_send, other_recv,
     parts_send, parts_recv, sums_send, sums_recv,
 ):
@@ -159,22 +159,17 @@
 
         lax.fori_loop(0, CHUNK // 16, some, 0, unroll=2)
 
-    def send_own(c):
-        @pl.when(seat != 0)
-        def _():
-            own_copy(chain, c).start()
-
     def send_late(n):
         for h in range(2):
             own_copy(side, chunk(CHUNKS - 1 - 2 * n - h)).start()
 
     normalise(chunk(0))
     pl.semaphore_wait(barrier, len(met))
-    send_own(chunk(0))
+    own_copy(chain, chunk(0)).start()
 
     def send_step(n, carry):
         normalise(chunk(n))
-        send_own(chunk(n))
+        own_copy(chain, chunk(n)).start()
         return carry
 
     lax.fori_loop(1, CHUNKS, send_step, 0)
@@ -195,7 +190,6 @@
     each_chunk(columns_of)
 
     mine = tags[S]
-    zero = jnp.zeros((CHUNKS, CHUNK), jnp.float32)
 
     def edge_tag(k):
         numbers = tags[REACH + k * way]
@@ -223,7 +217,12 @@
         edge = edge_tag(k)
         many = total_of(jnp.where(tags[REACH + k * way] == edge, 1.0, 0.0))
         counts = counts + jnp.where(mine == edge, many, 0.0)
+        masks[others.index(k)] = jnp.where(mine == edge, 1.0, 0.0)
     row_counts[...] = counts
+    first_tag = jnp.broadcast_to(mine[0:1, 0:1], (CHUNKS, CHUNK))
+    last_tag = jnp.broadcast_to(mine[CHUNKS - 1 : CHUNKS, CHUNK - 1 : CHUNK], (CHUNKS, CHUNK))
+    masks[len(others)] = jnp.where(mine == first_tag, 1.0, 0.0)
+    masks[len(others) + 1] = jnp.where(mine == last_tag, 1.0, 0.0)
 
     refs = {S: own, C1: near.at[chain], C2: far.at[chain], C3: third.at[chain], P1: near.at[side], P2: far.at[side], X: other}
 
@@ -259,11 +258,10 @@
         for h in range(2):
             c = chunk(2 * n + h)
             own_copy(chain, c).wait_recv()
-            relay_copy(chain, c).start()
-
-            @pl.when(seat == 0)
-            def _():
-                own_copy(chain, c).start()
+
+            @pl.when(seat != 0)
+            def _():
+                relay_copy(chain, c).start()
 
         @pl.when(d != 9)
         def _():
@@ -277,6 +275,10 @@
             for h in range(2):
                 c = chunk(2 * n + h)
                 relay_copy(chain, c).wait_recv()
+
+                @pl.when(seat == 0)
+                def _():
+                    relay_copy(chain, c).start()
 
                 @pl.when(passes_c2)
                 def _():
@@ -393,10 +395,8 @@
     )
     cover_ref[...] = cover
 
-    first_tag = jnp.broadcast_to(mine[0:1, 0:1], (CHUNKS, CHUNK))
-    last_tag = jnp.broadcast_to(mine[CHUNKS - 1 : CHUNKS, CHUNK - 1 : CHUNK], (CHUNKS, CHUNK))
-    sums[0] = total_of(jnp.where(mine == first_tag, cover, zero))
-    sums[1] = total_of(jnp.where(mine == last_tag, cover, zero))
+    for k in range(2):
+        sums[k] = total_of(masks[len(others) + k] * cover)
 
     def sums_copy(k):
         at = others.index(k)
@@ -409,7 +409,7 @@
     cluster_sums = own_totals(lambda c: row_sums[0, chunk_rows(c)])
     for k in others:
         sums_copy(k).wait_recv()
-        cluster_sums = cluster_sums + jnp.where(mine == edge_tag(-k), sums_in[others.index(k)], zero)
+        cluster_sums = cluster_sums + masks[others.index(-k)] * sums_in[others.index(k)]
     relative_ref[...] = cover - cluster_sums / row_counts[...]
 
     def sent(c):
@@ -458,6 +458,7 @@
             pltpu.VMEM((len(DOWN), rows, CHUNK), jnp.float32),
             pltpu.VMEM((len(ACROSS), CHUNKS, 8, CHUNK), jnp.float32),
             pltpu.VMEM(small, jnp.float32),
+            pltpu.VMEM((2 * REACH + 2, *small), jnp.float32),
             pltpu.VMEM(small, jnp.float32),
             pltpu.VMEM((len(PART_OFFSETS), *small), jnp.float32),
             pltpu.VMEM((len(PART_OFFSETS), *small), jnp.float32),

time: 110 us -> 101 us (0.918)
  Pallas kernels: 107 us -> 97.6 us
    pallas_call x1, Pallas kernels: 107 us -> 97.6 us  [per_device(): pl.pallas_call(kernel, out_shape=[jax.ShapeDtypeStruct(small, jnp.float32...]
where the time goes in v5:
time: 101 us
  Pallas kernels  97.6 us (97%)
  local copies, waits for them, and re-layouts  2.53 us (3%)
    pallas_call x1, Pallas kernels, per_device(): pl.pallas_call(kernel, out_shape=[jax.ShapeDtypeStruct(small, jnp.float32...  97.6 us
    unnamed x2, local copies, waits for them, and re-layouts  2.53 us

profile of v5, /device:TPU:32, one launch (start us, length us, event | category | flops | bytes accessed | tf_op | source)
XLA Modules:
  0.0 100.8 jit_solution(15722272047667497770)
XLA Ops:
  0.6 97.6 %cover.1 = (f32[8,128]{1,0:T(8,128)}, f32[8,128]{1,0:T(8,128)}) custom-call(bf16[1024,1024]{1,0:T(8,128)(2,1)} %x_ref.1, s32[256,8,128]{2,1,0:T(8,128)} %bitcast.3), custom_call_target="tpu_custom_call" | custom-call | tf_op jit(solution)/shard_map/cover/pallas_call | solution.py:444
  98.3 1.3 %copy.6 = f32[1024]{0:T(1024)} copy(f32[1024]{0:T(1024)} %bitcast.5) | data formatting | bytes 8192
  99.5 1.3 %copy.7 = f32[1024]{0:T(1024)} copy(f32[1024]{0:T(1024)} %bitcast.4) | data formatting | bytes 8192

commit v6 on v5

--- a/solution.py
+++ b/solution.py
@@ -252,117 +252,6 @@
 
         lax.fori_loop(first, last, some, 0)
 
-    each_pair(lambda c: strip(S, c, S))
-
-    def near_step(n):
-        for h in range(2):
-            c = chunk(2 * n + h)
-            own_copy(chain, c).wait_recv()
-
-            @pl.when(seat != 0)
-            def _():
-                relay_copy(chain, c).start()
-
-        @pl.when(d != 9)
-        def _():
-            strip(C1, pair(n), S)
-
-    each_pair(near_step)
-
-    @pl.when(has_c2)
-    def _():
-        def far_step(n):
-            for h in range(2):
-                c = chunk(2 * n + h)
-                relay_copy(chain, c).wait_recv()
-
-                @pl.when(seat == 0)
-                def _():
-                    relay_copy(chain, c).start()
-
-                @pl.when(passes_c2)
-                def _():
-                    relay2_copy(chain, c).start()
-
-                @pl.when(lends_c2)
-                def _():
-                    other_copy(c).start()
-
-            @pl.when((seat <= 2) & (n >= 2))
-            def _():
-                send_late(n - 2)
-
-            strip(C2, pair(n), S)
-
-        each_pair(far_step)
-
-    @pl.when(seat <= 2)
-    def _():
-        send_late(2)
-        send_late(3)
-
-    @pl.when(has_other)
-    def _():
-        def other_step(n):
-            last = PAIRS - 1 - n
-            for h in range(2):
-                other_copy(chunk(2 * last + 1 - h)).wait_recv()
-            pieces(last, PAIRS, X, lambda j: pair(last), C2, pair)
-
-        each_pair(other_step)
-
-    def side_step(n):
-        last = PAIRS - 1 - n
-        for h in range(2):
-            own_copy(side, chunk(2 * last + 1 - h)).wait_recv()
-        strip(P1, pair(last), C2)
-
-    @pl.when(first_seat)
-    def _():
-        def first_step(n):
-            side_step(n)
-            strip(P1, pair(PAIRS - 1 - n), C1)
-
-            @pl.when(d == 1)
-            def _():
-                strip(P1, pair(PAIRS - 1 - n), S)
-
-        each_pair(first_step)
-
-    @pl.when(has_c3)
-    def _():
-        def third_step(n):
-            last = PAIRS - 1 - n
-            for h in range(2):
-                relay2_copy(chain, chunk(2 * n + h)).wait_recv()
-
-            @pl.when(seat == 3)
-            def _():
-                strip(C3, pair(n), S)
-
-            @pl.when(has_other & (d != 13))
-            def _():
-                strip(C3, pair(n), X)
-
-            @pl.when(has_other)
-            def _():
-                side_step(n)
-
-            pieces(jnp.maximum(n, last), PAIRS, C3, lambda j: pair(n), P1, pair)
-            pieces(0, jnp.minimum(n, last + 1), C3, pair, P1, lambda j: pair(last))
-
-            @pl.when(first_seat)
-            def _():
-                for h in range(2):
-                    relay_copy(side, chunk(2 * last + 1 - h)).wait_recv()
-                pieces(n, PAIRS, P2, lambda j: pair(last), C2, lambda j: pair(PAIRS - 1 - j))
-
-                @pl.when(d == 1)
-                def _():
-                    strip(P2, pair(last), C1)
-
-        each_pair(third_step)
-
     def sums_of(kind):
         total = None
         if kind in ACROSS:
@@ -372,22 +261,181 @@
             total = total + jnp.concatenate([jnp.sum(jnp.transpose(r), axis=0, keepdims=True) for r in rows], axis=0)
         return total
 
-    parts[...] = jnp.zeros_like(parts)
-    for kind in (C1, C2, C3, P1, P2, X):
-        at = PART_OFFSETS.index(AWAY if kind == X else kind - REACH)
-        parts[jnp.where(leftward, at, len(PART_OFFSETS) - 1 - at)] = sums_of(kind)
+    def part_copy(kind):
+        offset = AWAY if kind == X else kind - REACH
+        at = PART_OFFSETS.index(offset)
+        at = jnp.where(leftward, at, len(PART_OFFSETS) - 1 - at)
+        return at, remote(parts.at[at], parts_in.at[at], parts_send.at[at], parts_recv.at[at], device(offset * way))
+
+    def send_part(kind):
+        at, copy = part_copy(kind)
+        parts[at] = sums_of(kind)
+        copy.start()
+
+    def part_comes(offset):
+        at = lax.rem(d + (PERIOD - offset), PERIOD)
+        left = (at >= 1) & (at <= 8)
+        there = jnp.where(left, at - 1, lax.rem(PERIOD - at, PERIOD))
+        rules = {1: there >= 0, 2: there <= 6, 3: there <= 3, -1: there <= 3, -2: there == 0, AWAY: (there >= 1) & (there <= 3)}
+        comes = []
+        if offset in rules:
+            comes.append(left & rules[offset])
+        if -offset in rules:
+            comes.append(jnp.logical_not(left) & rules[-offset])
+        return comes[0] if len(comes) == 1 else comes[0] | comes[1]
+
+    def chunks_sent(c):
+        own_copy(chain, c).wait_send()
+        relay_copy(chain, c).wait_send()
+
+        @pl.when(passes_own_back)
+        def _():
+            own_copy(side, c).wait_send()
+
+        @pl.when(passes_c2)
+        def _():
+            relay2_copy(chain, c).wait_send()
+
+        @pl.when(lends_c2)
+        def _():
+            other_copy(c).wait_send()
+
+    each_pair(lambda c: strip(S, c, S))
+
+    def near_step(n):
+        for h in range(2):
+            c = chunk(2 * n + h)
+            own_copy(chain, c).wait_recv()
+
+            @pl.when(seat != 0)
+            def _():
+                relay_copy(chain, c).start()
+
+        @pl.when(d != 9)
+        def _():
+            strip(C1, pair(n), S)
+
+    each_pair(near_step)
+
+    @pl.when(seat >= 1)
+    def _():
+        send_part(C1)
+
+    @pl.when(has_c2)
+    def _():
+        def far_step(n):
+            for h in range(2):
+                c = chunk(2 * n + h)
+                relay_copy(chain, c).wait_recv()
+
+                @pl.when(seat == 0)
+                def _():
+                    relay_copy(chain, c).start()
+
+                @pl.when(passes_c2)
+                def _():
+                    relay2_copy(chain, c).start()
+
+                @pl.when(lends_c2)
+                def _():
+                    other_copy(c).start()
+
+            @pl.when((seat <= 2) & (n >= 2))
+            def _():
+                send_late(n - 2)
+
+            strip(C2, pair(n), S)
+
+        each_pair(far_step)
+
+        @pl.when(seat >= 4)
+        def _():
+            send_part(C2)
+
+    @pl.when(seat <= 2)
+    def _():
+        send_late(2)
+        send_late(3)
+
+    @pl.when(has_other)
+    def _():
+        def other_step(n):
+            last = PAIRS - 1 - n
+            for h in range(2):
+                other_copy(chunk(2 * last + 1 - h)).wait_recv()
+            pieces(last, PAIRS, X, lambda j: pair(last), C2, pair)
+
+        each_pair(other_step)
+
+    def side_step(n):
+        last = PAIRS - 1 - n
+        for h in range(2):
+            own_copy(side, chunk(2 * last + 1 - h)).wait_recv()
+        strip(P1, pair(last), C2)
+
+    @pl.when(first_seat)
+    def _():
+        def first_step(n):
+            side_step(n)
+            strip(P1, pair(PAIRS - 1 - n), C1)
+
+            @pl.when(d == 1)
+            def _():
+                strip(P1, pair(PAIRS - 1 - n), S)
+
+        each_pair(first_step)
+
+    @pl.when(has_c3)
+    def _():
+        def third_step(n):
+            last = PAIRS - 1 - n
+            for h in range(2):
+                relay2_copy(chain, chunk(2 * n + h)).wait_recv()
+
+            @pl.when(seat == 3)
+            def _():
+                strip(C3, pair(n), S)
+
+            @pl.when(has_other & (d != 13))
+            def _():
+                strip(C3, pair(n), X)
+
+            @pl.when(has_other)
+            def _():
+                side_step(n)
+
+            pieces(jnp.maximum(n, last), PAIRS, C3, lambda j: pair(n), P1, pair)
+            pieces(0, jnp.minimum(n, last + 1), C3, pair, P1, lambda j: pair(last))
+
+            @pl.when(first_seat)
+            def _():
+                for h in range(2):
+                    relay_copy(side, chunk(2 * last + 1 - h)).wait_recv()
+                pieces(n, PAIRS, P2, lambda j: pair(last), C2, lambda j: pair(PAIRS - 1 - j))
+
+                @pl.when(d == 1)
+                def _():
+                    strip(P2, pair(last), C1)
+
+        each_pair(third_step)
+
+    for kind, sends in ((C1, first_seat), (C2, has_c2 & (seat <= 3)), (C3, has_c3), (P1, has_p1), (P2, first_seat), (X, has_other)):
+
+        @pl.when(sends)
+        def _():
+            send_part(kind)
+
     own_part[...] = sums_of(S)
-
-    def parts_copy(k):
-        return remote(parts.at[k], parts_in.at[k], parts_send.at[k], parts_recv.at[k], device(PART_OFFSETS[k]))
-
-    for k in range(len(PART_OFFSETS)):
-        parts_copy(k).start()
+    each_chunk(chunks_sent)
+
+    for k, offset in enumerate(PART_OFFSETS):
+
+        @pl.when(part_comes(offset))
+        def _():
+            remote(parts.at[k], parts_in.at[k], parts_send.at[k], parts_recv.at[k], device(offset)).wait_recv()
+            own_part[...] += parts_in[k]
 
     total = own_part[...]
-    for k in range(len(PART_OFFSETS)):
-        parts_copy(k).wait_recv()
-        total = total + parts_in[k]
     cover = jnp.where(
         total < math.exp(-SHIFT),
         jnp.log1p(jnp.minimum(total, math.exp(-SHIFT)) * math.exp(SHIFT)),
@@ -404,6 +452,12 @@
 
     for k in others:
         sums_copy(k).start()
+    for kind, sends in ((C1, seat >= 0), (C2, has_c2), (C3, has_c3), (P1, has_p1), (P2, first_seat), (X, has_other)):
+
+        @pl.when(sends)
+        def _():
+            part_copy(kind)[1].wait_send()
+
     for c in range(CHUNKS):
         row_sums[0, c * CHUNK : (c + 1) * CHUNK] = across(cover[c : c + 1])
     cluster_sums = own_totals(lambda c: row_sums[0, chunk_rows(c)])
@@ -412,25 +466,6 @@
         cluster_sums = cluster_sums + masks[others.index(-k)] * sums_in[others.index(k)]
     relative_ref[...] = cover - cluster_sums / row_counts[...]
 
-    def sent(c):
-        own_copy(chain, c).wait_send()
-        relay_copy(chain, c).wait_send()
-
-        @pl.when(passes_own_back)
-        def _():
-            own_copy(side, c).wait_send()
-
-        @pl.when(passes_c2)
-        def _():
-            relay2_copy(chain, c).wait_send()
-
-        @pl.when(lends_c2)
-        def _():
-            other_copy(c).wait_send()
-
-    each_chunk(sent)
-    for k in range(len(PART_OFFSETS)):
-        parts_copy(k).wait_send()
     for k in others:
         sums_copy(k).wait_send()
 
@@ -480,7 +515,7 @@
             dma((2 * REACH,)),
         ],
         compiler_params=pltpu.CompilerParams(
-            collective_id=0, has_side_effects=True, vmem_limit_bytes=60 << 20
+            collective_id=0, has_side_effects=True, vmem_limit_bytes=53 << 20
         ),
         name="cover",
     )(embeddings, cluster.reshape(-1, *small))

time: 101 us -> 97.7 us (0.967)
  Pallas kernels: 97.6 us -> 95.6 us
  local copies, waits for them, and re-layouts: 2.53 us -> 1.19 us
    pallas_call x1, Pallas kernels: 97.6 us -> 95.6 us  [per_device(): pl.pallas_call(kernel, out_shape=[jax.ShapeDtypeStruct(small, jnp.float32...]
    unnamed x2, local copies, waits for them, and re-layouts: 2.53 us -> 1.19 us
where the time goes in v6:
time: 97.7 us; the launch traced here: 97.4 us
  Pallas kernels  95.6 us (98%)
  local copies, waits for them, and re-layouts  1.19 us (1%)
    pallas_call x1, Pallas kernels, per_device(): pl.pallas_call(kernel, out_shape=[jax.ShapeDtypeStruct(small, jnp.float32...  95.6 us

profile of v6, /device:TPU:32, one launch (start us, length us, event | category | flops | bytes accessed | tf_op | source)
XLA Modules:
  0.0 97.4 jit_solution(16423809855304190666)
XLA Ops:
  0.6 95.6 %cover.1 = (f32[8,128]{1,0:T(8,128)S(1)}, f32[8,128]{1,0:T(8,128)S(1)}) custom-call(bf16[1024,1024]{1,0:T(8,128)(2,1)} %x_ref.1, s32[256,8,128]{2,1,0:T(8,128)} %bitcast.5), custom_call_target="tpu_custom_call" | custom-call | tf_op jit(solution)/shard_map/cover/pallas_call | solution.py:479
  96.2 0.6 copy.6
  96.8 0.6 copy.7

commit v7 on v6

--- a/solution.py
+++ b/solution.py
@@ -46,6 +46,14 @@
     return lax.dot_general(left, right, (((1,), (1,)), ((), ())), preferred_element_type=jnp.float32)
 
 
+def log_of(total):
+    return jnp.where(
+        total < math.exp(-SHIFT),
+        jnp.log1p(jnp.minimum(total, math.exp(-SHIFT)) * math.exp(SHIFT)),
+        SHIFT + jnp.log(total + math.exp(-SHIFT)),
+    )
+
+
 def each_chunk(body):
     def step(c, carry):
         body(c)
@@ -63,7 +71,7 @@
 
 
 def kernel(
-    x_ref, cluster_ref, cover_ref, relative_ref,
+    x_ref, cluster_ref, total_ref, mean_ref,
     raw, own, near, far, third, other, tags, columns, row_sums, col_sums, row_counts, masks, own_part, parts, parts_in, sums, sums_in,
     raw_sem, tags_sem, own_send, near_recv, relay_send, far_recv, relay2_send, third_recv, other_send, other_recv,
     parts_send, parts_recv, sums_send, sums_recv,
@@ -419,7 +427,7 @@
 
         each_pair(third_step)
 
-    for kind, sends in ((C1, first_seat), (C2, has_c2 & (seat <= 3)), (C3, has_c3), (P1, has_p1), (P2, first_seat), (X, has_other)):
+    for kind, sends in ((X, has_other), (C3, has_c3), (P2, first_seat), (C2, has_c2 & (seat <= 3)), (P1, has_p1), (C1, first_seat)):
 
         @pl.when(sends)
         def _():
@@ -436,12 +444,8 @@
             own_part[...] += parts_in[k]
 
     total = own_part[...]
-    cover = jnp.where(
-        total < math.exp(-SHIFT),
-        jnp.log1p(jnp.minimum(total, math.exp(-SHIFT)) * math.exp(SHIFT)),
-        SHIFT + jnp.log(total + math.exp(-SHIFT)),
-    )
-    cover_ref[...] = cover
+    cover = log_of(total)
+    total_ref[...] = total
 
     for k in range(2):
         sums[k] = total_of(masks[len(others) + k] * cover)
@@ -450,7 +454,7 @@
         at = others.index(k)
         return remote(sums.at[0 if k < 0 else 1], sums_in.at[at], sums_send.at[at], sums_recv.at[at], device(k))
 
-    for k in others:
+    for k in sorted(others, key=abs, reverse=True):
         sums_copy(k).start()
     for kind, sends in ((C1, seat >= 0), (C2, has_c2), (C3, has_c3), (P1, has_p1), (P2, first_seat), (X, has_other)):
 
@@ -464,7 +468,7 @@
     for k in others:
         sums_copy(k).wait_recv()
         cluster_sums = cluster_sums + masks[others.index(-k)] * sums_in[others.index(k)]
-    relative_ref[...] = cover - cluster_sums / row_counts[...]
+    mean_ref[...] = cluster_sums / row_counts[...]
 
     for k in others:
         sums_copy(k).wait_send()
@@ -476,7 +480,7 @@
     hbm = pl.BlockSpec(memory_space=pltpu.HBM)
     dma = pltpu.SemaphoreType.DMA
     small = (CHUNKS, CHUNK)
-    cover, relative = pl.pallas_call(
+    total, mean = pl.pallas_call(
         kernel,
         out_shape=[jax.ShapeDtypeStruct(small, jnp.float32)] * 2,
         in_specs=[hbm, hbm],
@@ -519,7 +523,8 @@
         ),
         name="cover",
     )(embeddings, cluster.reshape(-1, *small))
-    return cover.reshape(rows), relative.reshape(rows)
+    cover = log_of(total.reshape(rows))
+    return cover, cover - mean.reshape(rows)
 
 
 def solution(mesh):

time: 97.7 us -> 96.7 us (0.990)
  local copies, waits for them, and re-layouts: 1.19 us -> 0 us
    unnamed x2 -> x0, local copies, waits for them, and re-layouts: 1.19 us -> none
where the time goes in v7:
time: 96.7 us; the launch traced here: 96.2 us
  Pallas kernels  94.9 us (98%)
    pallas_call x1, Pallas kernels, per_device(): pl.pallas_call(kernel, out_shape=[jax.ShapeDtypeStruct(small, jnp.float32...  94.9 us

profile of v7, /device:TPU:32, one launch (start us, length us, event | category | flops | bytes accessed | tf_op | source)
XLA Modules:
  0.0 96.2 jit_solution(4963249699602232515)
XLA Ops:
  0.6 94.9 %cover.1 = (f32[8,128]{1,0:T(8,128)S(1)}, f32[8,128]{1,0:T(8,128)S(1)}) custom-call(bf16[1024,1024]{1,0:T(8,128)(2,1)} %x_ref.1, s32[256,8,128]{2,1,0:T(8,128)} %bitcast.6), custom_call_target="tpu_custom_call" | custom-call | tf_op jit(solution)/shard_map/cover/pallas_call | solution.py:483
  95.6 0.6 bitcast_subtract_fusion

commit v8 on v7

--- a/solution.py
+++ b/solution.py
@@ -145,15 +145,16 @@
         rows = chunk_rows(c)
         return remote(far.at[chain, rows], other.at[rows], other_send.at[c], other_recv.at[c], other_core)
 
-    each_chunk(lambda n: raw_copy(chunk(n)).start())
-    for k in range(2 * REACH + 2):
-        tags_copy(k).start()
-
+    raw_copy(chunk(0)).start()
     barrier = pltpu.get_barrier_semaphore()
     others = [k for k in range(-REACH, REACH + 1) if k != 0]
     met = [device(k) for k in others + [-AWAY, AWAY]] + [other_core]
     for to in met:
         pl.semaphore_signal(barrier, inc=1, device_id=to, device_id_type=MESH)
+    for n in range(1, CHUNKS):
+        raw_copy(chunk(n)).start()
+    for k in range(2 * REACH + 2):
+        tags_copy(k).start()
 
     def normalise(c):
         raw_copy(c).wait()
@@ -408,12 +409,21 @@
             def _():
                 strip(C3, pair(n), X)
 
+            @pl.when(has_other & (n == PAIRS - 1))
+            def _():
+                send_part(X)
+
             @pl.when(has_other)
             def _():
                 side_step(n)
 
             pieces(jnp.maximum(n, last), PAIRS, C3, lambda j: pair(n), P1, pair)
             pieces(0, jnp.minimum(n, last + 1), C3, pair, P1, lambda j: pair(last))
+
+            @pl.when(first_seat & (n == PAIRS - 1))
+            def _():
+                send_part(C3)
+                send_part(P1)
 
             @pl.when(first_seat)
             def _():
@@ -427,7 +437,7 @@
 
         each_pair(third_step)
 
-    for kind, sends in ((X, has_other), (C3, has_c3), (P2, first_seat), (C2, has_c2 & (seat <= 3)), (P1, has_p1), (C1, first_seat)):
+    for kind, sends in ((C3, has_other), (P2, first_seat), (C2, has_c2 & (seat <= 3)), (P1, has_other), (C1, first_seat)):
 
         @pl.when(sends)
         def _():
@@ -452,7 +462,7 @@
 
     def sums_copy(k):
         at = others.index(k)
-        return remote(sums.at[0 if k < 0 else 1], sums_in.at[at], sums_send.at[at], sums_recv.at[at], device(k))
+        return remote(sums.at[0 if k < 0 else 1, 0:1], sums_in.at[at, 0:1], sums_send.at[at], sums_recv.at[at], device(k))
 
     for k in sorted(others, key=abs, reverse=True):
         sums_copy(k).start()
@@ -467,7 +477,7 @@
     cluster_sums = own_totals(lambda c: row_sums[0, chunk_rows(c)])
     for k in others:
         sums_copy(k).wait_recv()
-        cluster_sums = cluster_sums + masks[others.index(-k)] * sums_in[others.index(k)]
+        cluster_sums = cluster_sums + masks[others.index(-k)] * sums_in[others.index(k), 0:1]
     mean_ref[...] = cluster_sums / row_counts[...]
 
     for k in others:

time: 96.7 us -> 96.3 us (level)
  no operation moved by 1% of the time
where the time goes in v8:
time: 96.3 us; the launch traced here: 96.2 us
  Pallas kernels  95 us (99%)
    pallas_call x1, Pallas kernels, per_device(): pl.pallas_call(kernel, out_shape=[jax.ShapeDtypeStruct(small, jnp.float32...  95 us

profile of v8, /device:TPU:32, one launch (start us, length us, event | category | flops | bytes accessed | tf_op | source)
XLA Modules:
  0.0 96.2 jit_solution(499167220415073919)
XLA Ops:
  0.6 95.0 %cover.1 = (f32[8,128]{1,0:T(8,128)S(1)}, f32[8,128]{1,0:T(8,128)S(1)}) custom-call(bf16[1024,1024]{1,0:T(8,128)(2,1)} %x_ref.1, s32[256,8,128]{2,1,0:T(8,128)} %bitcast.6), custom_call_target="tpu_custom_call" | custom-call | tf_op jit(solution)/shard_map/cover/pallas_call | solution.py:493
  95.6 0.6 bitcast_subtract_fusion

commit v9 on v8

--- a/solution.py
+++ b/solution.py
@@ -295,7 +295,9 @@
 
     def chunks_sent(c):
         own_copy(chain, c).wait_send()
-        relay_copy(chain, c).wait_send()
+        @pl.when(jnp.logical_not(passes_c2))
+        def _():
+            relay_copy(chain, c).wait_send()
 
         @pl.when(passes_own_back)
         def _():
@@ -310,6 +312,16 @@
             other_copy(c).wait_send()
 
     each_pair(lambda c: strip(S, c, S))
+
+    def after_relay(n, ahead):
+        @pl.when(n == 0)
+        def _():
+            for early in range(ahead):
+                relay_copy(chain, chunk(early)).wait_send()
+
+        @pl.when(n + ahead < CHUNKS)
+        def _():
+            relay_copy(chain, chunk(n + ahead)).wait_send()
 
     def near_step(n):
         for h in range(2):
@@ -343,6 +355,7 @@
 
                 @pl.when(passes_c2)
                 def _():
+                    after_relay(2 * n + h, 2)
                     relay2_copy(chain, c).start()
 
                 @pl.when(lends_c2)

time: 96.3 us -> 96.3 us (level)
  no operation moved by 1% of the time
where the time goes in v9:
time: 96.3 us; the launch traced here: 96.2 us
  Pallas kernels  95 us (99%)
    pallas_call x1, Pallas kernels, per_device(): pl.pallas_call(kernel, out_shape=[jax.ShapeDtypeStruct(small, jnp.float32...  95 us

profile of v9, /device:TPU:32, one launch (start us, length us, event | category | flops | bytes accessed | tf_op | source)
XLA Modules:
  0.0 96.2 jit_solution(4253934650920766509)
XLA Ops:
  0.6 95.0 %cover.1 = (f32[8,128]{1,0:T(8,128)S(1)}, f32[8,128]{1,0:T(8,128)S(1)}) custom-call(bf16[1024,1024]{1,0:T(8,128)(2,1)} %x_ref.1, s32[256,8,128]{2,1,0:T(8,128)} %bitcast.6), custom_call_target="tpu_custom_call" | custom-call | tf_op jit(solution)/shard_map/cover/pallas_call | solution.py:506
  95.6 0.6 bitcast_subtract_fusion

commit v10 on v8

--- a/solution.py
+++ b/solution.py
@@ -166,7 +166,7 @@
             own[rows] = (values * scale).astype(jnp.bfloat16)
             return carry
 
-        lax.fori_loop(0, CHUNK // 16, some, 0, unroll=2)
+        lax.fori_loop(0, CHUNK // 16, some, 0, unroll=True)
 
     def send_late(n):
         for h in range(2):

time: 96.3 us -> 96.3 us (level)
  no operation moved by 1% of the time
where the time goes in v10:
time: 96.3 us; the launch traced here: 96.2 us
  Pallas kernels  95 us (99%)
    pallas_call x1, Pallas kernels, per_device(): pl.pallas_call(kernel, out_shape=[jax.ShapeDtypeStruct(small, jnp.float32...  95 us

profile of v10, /device:TPU:32, one launch (start us, length us, event | category | flops | bytes accessed | tf_op | source)
XLA Modules:
  0.0 96.2 jit_solution(8271783769870860566)
XLA Ops:
  0.6 95.0 %cover.1 = (f32[8,128]{1,0:T(8,128)S(1)}, f32[8,128]{1,0:T(8,128)S(1)}) custom-call(bf16[1024,1024]{1,0:T(8,128)(2,1)} %x_ref.1, s32[256,8,128]{2,1,0:T(8,128)} %bitcast.6), custom_call_target="tpu_custom_call" | custom-call | tf_op jit(solution)/shard_map/cover/pallas_call | solution.py:493
  95.6 0.6 bitcast_subtract_fusion
